TPU v7x, 32 devices: a whole 2x2x4 slice. The times are simulated.
32 devices in a mesh: pos: 16 (over z, y, x), clip: 2 (over core).
Axes of the slice: x: 2, y: 2, z: 4, core: 2. Of those that a mesh axis runs over, the one named last changes fastest.
Arguments:
- tokens: bfloat16 [4, 16, 1024, 384], P('clip', None, 'pos'), may hold values from -18 to 18
- timesteps: int32 [4], P('clip'), may hold values from 0 to 999
- weight_codes: int32 [4], P('clip'), may hold values from 0 to 7
- cotangent: bfloat16 [4, 16, 1024, 384], P('clip', None, 'pos'), may hold values from -6 to 6
- ada_weight: bfloat16 [2, 384, 2304], replicated, may hold values from -0.3125 to 0.3125
- qkv_weight: bfloat16 [2, 384, 1152], replicated, may hold values from -0.3125 to 0.3125
- out_weight: bfloat16 [2, 384, 384], replicated, may hold values from -2.5 to 2.5
- up_weight: bfloat16 [2, 384, 1536], replicated, may hold values from -0.3125 to 0.3125
- down_weight: bfloat16 [2, 1536, 384], replicated, may hold values from -0.15625 to 0.15625
Outputs:
- activations: bfloat16 [4, 16, 1024, 384], P('clip', None, 'pos')
- grad_tokens: float32 [4, 16, 1024, 384], P('clip', None, 'pos')
- ada_grad: float32 [2, 384, 2304], replicated
- qkv_grad: float32 [2, 384, 1152], replicated
- out_grad: float32 [2, 384, 384], replicated
- up_grad: float32 [2, 384, 1536], replicated
- down_grad: float32 [2, 1536, 384], replicated
- stream_rms: float32 [2, 3], replicated
All inputs are finite; a program needn't handle non-finite values.
Results may differ from a plain program's by a relative error of at most 0.017.
Values may be sent and summed in bfloat16 or wider, within the bound.
No kernel may reach another device: no remote copies, remote signals or barrier semaphores. Data moves between devices by JAX's collectives and lax.ppermute only.
A program may use at most 512 MiB of HBM per device.

v0:
```python
from functools import partial
import math

import jax
import jax.numpy as jnp
from jax import lax
from jax.sharding import PartitionSpec as P

D = 384
HEADS = 6
HEAD = 64
BLOCKS = 2


EPS = 1e-06


def layer_norm(values):
    center = values - jnp.mean(values, axis=-1, keepdims=True)
    spread = jnp.mean(center * center, axis=-1, keepdims=True)
    return center * lax.rsqrt(spread + EPS)


def modulate(values, shift_part, scale_part):
    return layer_norm(values) * (1.0 + scale_part[:, None, None, :]) + shift_part[:, None, None, :]


def embed_steps(timesteps):
    half_width = D // 2
    frequencies = jnp.exp(
        -math.log(10000.0) * jnp.arange(half_width, dtype=jnp.float32) / half_width
    )
    angles = timesteps.astype(jnp.float32)[:, None] * frequencies[None, :]
    return jax.nn.silu(jnp.concatenate([jnp.cos(angles), jnp.sin(angles)], axis=-1))


def split_heads(values):
    return values.reshape(values.shape[:-1] + (HEADS, HEAD))


def merge_heads(values):
    return values.reshape(values.shape[:-2] + (HEADS * HEAD,))


def outer_sum(left_rows, right_rows):
    left_flat = left_rows.reshape(-1, left_rows.shape[-1])
    right_flat = right_rows.reshape(-1, right_rows.shape[-1])
    return lax.dot_general(
        left_flat, right_flat, (((0,), (0,)), ((), ())), preferred_element_type=jnp.float32
    )


def back_dense(grad_rows, weight):
    return lax.dot_general(
        grad_rows,
        weight,
        (((grad_rows.ndim - 1,), (1,)), ((), ())),
        preferred_element_type=jnp.float32,
    )


def attend_forward(query_heads, key_heads, value_heads, score_spec, mix_spec):
    scores = jnp.einsum(
        score_spec, query_heads, key_heads, preferred_element_type=jnp.float32
    ) * HEAD ** (-0.5)
    largest = jnp.max(scores, axis=-1, keepdims=True)
    raised = jnp.exp(scores - largest)
    totals = jnp.sum(raised, axis=-1, keepdims=True)
    attn_probs = (raised / totals).astype(jnp.bfloat16)
    mixed_heads = jnp.einsum(mix_spec, attn_probs, value_heads, preferred_element_type=jnp.float32)
    return (merge_heads(mixed_heads).astype(jnp.bfloat16), largest + jnp.log(totals))


def attend_backward(
    query_heads, key_heads, value_heads, log_totals, grad_heads, score_spec, mix_spec
):
    scores = jnp.einsum(
        score_spec, query_heads, key_heads, preferred_element_type=jnp.float32
    ) * HEAD ** (-0.5)
    attn_probs = jnp.exp(scores - log_totals)
    grad_probs = jnp.einsum(score_spec, grad_heads, value_heads, preferred_element_type=jnp.float32)
    row_terms = jnp.sum(grad_probs * attn_probs, axis=-1, keepdims=True)
    grad_scores = (attn_probs * (grad_probs - row_terms)).astype(jnp.bfloat16)
    grad_query = jnp.einsum(
        mix_spec, grad_scores, key_heads, preferred_element_type=jnp.float32
    ) * HEAD ** (-0.5)
    return (grad_query, grad_scores, attn_probs.astype(jnp.bfloat16))


def spatial_forward(projected):
    third_width = projected.shape[-1] // 3
    framed = lax.all_to_all(projected, "pos", split_axis=0, concat_axis=1, tiled=True)
    mixed_rows, log_totals = attend_forward(
        split_heads(framed[..., :third_width]),
        split_heads(framed[..., third_width : 2 * third_width]),
        split_heads(framed[..., 2 * third_width :]),
        "bqhd,bkhd->bhqk",
        "bhqk,bkhd->bqhd",
    )
    attended = lax.all_to_all(mixed_rows, "pos", split_axis=1, concat_axis=0, tiled=True)
    return (attended, (framed, log_totals))


def spatial_backward(projected, saved_state, grad_attended):
    third_width = projected.shape[-1] // 3
    framed, log_totals = saved_state
    grad_framed = lax.all_to_all(grad_attended, "pos", split_axis=0, concat_axis=1, tiled=True)
    query_heads = split_heads(framed[..., :third_width])
    grad_heads = split_heads(grad_framed)
    grad_query, grad_scores, probs_low = attend_backward(
        query_heads,
        split_heads(framed[..., third_width : 2 * third_width]),
        split_heads(framed[..., 2 * third_width :]),
        log_totals,
        grad_heads,
        "bqhd,bkhd->bhqk",
        "bhqk,bkhd->bqhd",
    )
    grad_keys = jnp.einsum(
        "bhqk,bqhd->bkhd", grad_scores, query_heads, preferred_element_type=jnp.float32
    ) * HEAD ** (-0.5)
    grad_values = jnp.einsum(
        "bhqk,bqhd->bkhd", probs_low, grad_heads, preferred_element_type=jnp.float32
    )
    grad_local = jnp.concatenate(
        [merge_heads(grad_query), merge_heads(grad_keys), merge_heads(grad_values)], axis=-1
    ).astype(jnp.bfloat16)
    return lax.all_to_all(grad_local, "pos", split_axis=1, concat_axis=0, tiled=True)


def temporal_forward(projected):
    third_width = projected.shape[-1] // 3
    return attend_forward(
        split_heads(projected[..., :third_width]),
        split_heads(projected[..., third_width : 2 * third_width]),
        split_heads(projected[..., 2 * third_width :]),
        "cqphd,ckphd->cphqk",
        "cphqk,ckphd->cqphd",
    )


def temporal_backward(projected, log_totals, grad_attended):
    third_width = projected.shape[-1] // 3
    query_heads = split_heads(projected[..., :third_width])
    grad_heads = split_heads(grad_attended)
    grad_query, grad_scores, probs_low = attend_backward(
        query_heads,
        split_heads(projected[..., third_width : 2 * third_width]),
        split_heads(projected[..., 2 * third_width :]),
        log_totals,
        grad_heads,
        "cqphd,ckphd->cphqk",
        "cphqk,ckphd->cqphd",
    )
    grad_keys = jnp.einsum(
        "cphqk,cqphd->ckphd", grad_scores, query_heads, preferred_element_type=jnp.float32
    ) * HEAD ** (-0.5)
    grad_values = jnp.einsum(
        "cphqk,cqphd->ckphd", probs_low, grad_heads, preferred_element_type=jnp.float32
    )
    return jnp.concatenate(
        [merge_heads(grad_query), merge_heads(grad_keys), merge_heads(grad_values)], axis=-1
    ).astype(jnp.bfloat16)


def block_forward(stream, modulation, qkv_matrix, out_matrix, up_matrix, down_matrix, across):
    mod_parts = jnp.split(modulation, 6, axis=-1)
    hidden = modulate(stream, mod_parts[0], mod_parts[1]).astype(jnp.bfloat16)
    projected = jnp.dot(hidden, qkv_matrix, preferred_element_type=jnp.float32).astype(jnp.bfloat16)
    if across:
        frame_rows = projected.reshape((-1,) + projected.shape[2:])
        attended, saved_state = spatial_forward(frame_rows)
        attended = attended.reshape(stream.shape)
    else:
        attended, saved_state = temporal_forward(projected)
    branch_out = jnp.dot(attended, out_matrix, preferred_element_type=jnp.float32)
    attn_branch = mod_parts[2][:, None, None, :] * branch_out
    middle = stream + attn_branch
    hidden_two = modulate(middle, mod_parts[3], mod_parts[4]).astype(jnp.bfloat16)
    inner_rows = jnp.dot(hidden_two, up_matrix, preferred_element_type=jnp.float32)
    activated = jax.nn.gelu(inner_rows, approximate=True).astype(jnp.bfloat16)
    mlp_out = jnp.dot(activated, down_matrix, preferred_element_type=jnp.float32)
    mlp_branch = mod_parts[5][:, None, None, :] * mlp_out
    squares = jnp.stack(
        [
            jnp.sum(stream * stream),
            jnp.sum(attn_branch * attn_branch),
            jnp.sum(mlp_branch * mlp_branch),
        ]
    )
    kept_values = (
        stream,
        hidden,
        projected,
        saved_state,
        attended,
        branch_out,
        middle,
        hidden_two,
        inner_rows,
        activated,
        mlp_out,
    )
    return (middle + mlp_branch, squares, kept_values)


def block_backward(
    grad_stream, modulation, kept_values, qkv_matrix, out_matrix, up_matrix, down_matrix, across
):
    (
        stream,
        hidden,
        projected,
        saved_state,
        attended,
        branch_out,
        middle,
        hidden_two,
        inner_rows,
        activated,
        mlp_out,
    ) = kept_values
    mod_parts = jnp.split(modulation, 6, axis=-1)
    grad_gate_two = jnp.sum(mlp_out * grad_stream, axis=(1, 2))
    grad_mlp = (mod_parts[5][:, None, None, :] * grad_stream).astype(jnp.bfloat16)
    down_part = outer_sum(activated, grad_mlp)
    grad_act = back_dense(grad_mlp, down_matrix)
    gelu_tanh = partial(jax.nn.gelu, approximate=True)
    grad_inner = jax.vjp(gelu_tanh, inner_rows)[1](grad_act)[0].astype(jnp.bfloat16)
    up_part = outer_sum(hidden_two, grad_inner)
    grad_hidden_two = back_dense(grad_inner, up_matrix)
    norm_back_two = jax.vjp(modulate, middle, mod_parts[3], mod_parts[4])[1]
    grad_middle_norm, grad_shift_two, grad_scale_two = norm_back_two(grad_hidden_two)
    grad_middle = grad_stream + grad_middle_norm
    grad_gate_one = jnp.sum(branch_out * grad_middle, axis=(1, 2))
    grad_branch = (mod_parts[2][:, None, None, :] * grad_middle).astype(jnp.bfloat16)
    out_part = outer_sum(attended, grad_branch)
    grad_attended = back_dense(grad_branch, out_matrix).astype(jnp.bfloat16)
    if across:
        frame_shape = (-1,) + projected.shape[2:]
        grad_projected = spatial_backward(
            projected.reshape(frame_shape),
            saved_state,
            grad_attended.reshape((-1,) + grad_attended.shape[2:]),
        )
        grad_projected = grad_projected.reshape(projected.shape)
    else:
        grad_projected = temporal_backward(projected, saved_state, grad_attended)
    qkv_part = outer_sum(hidden, grad_projected)
    grad_hidden = back_dense(grad_projected, qkv_matrix)
    norm_back_one = jax.vjp(modulate, stream, mod_parts[0], mod_parts[1])[1]
    grad_stream_norm, grad_shift_one, grad_scale_one = norm_back_one(grad_hidden)
    grad_modulation = jnp.concatenate(
        [
            grad_shift_one,
            grad_scale_one,
            grad_gate_one,
            grad_shift_two,
            grad_scale_two,
            grad_gate_two,
        ],
        axis=-1,
    )
    return (
        grad_middle + grad_stream_norm,
        grad_modulation,
        (qkv_part, out_part, up_part, down_part),
    )


def on_device(
    tokens,
    timesteps,
    weight_codes,
    cotangent,
    ada_weight,
    qkv_weight,
    out_weight,
    up_weight,
    down_weight,
):
    embedded = embed_steps(timesteps)
    stream = tokens.astype(jnp.float32)
    modulations = []
    kept_all = []
    squares_all = []
    for block_index in range(BLOCKS):
        modulation = jnp.dot(
            embedded, ada_weight[block_index].astype(jnp.float32), precision=lax.Precision.HIGHEST
        )
        stream, squares, kept_values = block_forward(
            stream,
            modulation,
            qkv_weight[block_index],
            out_weight[block_index],
            up_weight[block_index],
            down_weight[block_index],
            block_index % 2 == 0,
        )
        modulations.append(modulation)
        kept_all.append(kept_values)
        squares_all.append(squares)
    activations = stream.astype(jnp.bfloat16)
    squares_local = jnp.stack(squares_all)
    squares_total = lax.psum(squares_local, ("pos", "clip"))
    scaling = jnp.exp2(0.5 * weight_codes.astype(jnp.float32) - 1.0)
    grad_stream = cotangent.astype(jnp.float32) * scaling[:, None, None, None]
    mod_grads = [None] * BLOCKS
    weight_terms = [None] * BLOCKS
    for block_index in reversed(range(BLOCKS)):
        grad_stream, mod_grads[block_index], weight_terms[block_index] = block_backward(
            grad_stream,
            modulations[block_index],
            kept_all[block_index],
            qkv_weight[block_index],
            out_weight[block_index],
            up_weight[block_index],
            down_weight[block_index],
            block_index % 2 == 0,
        )
    mod_local = jnp.stack(mod_grads, axis=1)
    mod_total = lax.psum(mod_local.astype(jnp.bfloat16), "pos").astype(jnp.float32)
    mod_rows, embed_rows = (
        lax.all_gather(mod_total.astype(jnp.bfloat16), "clip", axis=0, tiled=True).astype(
            mod_total.dtype
        ),
        lax.all_gather(embedded.astype(jnp.bfloat16), "clip", axis=0, tiled=True).astype(
            embedded.dtype
        ),
    )
    ada_grad = jnp.einsum("cd,cbe->bde", embed_rows, mod_rows, precision=lax.Precision.HIGHEST)
    qkv_local = jnp.stack([terms[0] for terms in weight_terms])
    out_local = jnp.stack([terms[1] for terms in weight_terms])
    up_local = jnp.stack([terms[2] for terms in weight_terms])
    down_local = jnp.stack([terms[3] for terms in weight_terms])
    summed = lax.psum((qkv_local, out_local, up_local, down_local), ("pos", "clip"))
    token_count = (
        tokens.shape[0]
        * tokens.shape[1]
        * tokens.shape[2]
        * lax.axis_size("pos")
        * lax.axis_size("clip")
    )
    stream_rms = jnp.sqrt(squares_total / token_count)
    return (
        activations,
        grad_stream,
        ada_grad,
        summed[0],
        summed[1],
        summed[2],
        summed[3],
        stream_rms,
    )


def solution(mesh):
    placed = (
        P("clip", None, "pos", None),
        P("clip"),
        P("clip"),
        P("clip", None, "pos", None),
        P(),
        P(),
        P(),
        P(),
        P(),
    )
    return jax.shard_map(
        on_device,
        mesh=mesh,
        in_specs=placed,
        out_specs=(
            P("clip", None, "pos", None),
            P("clip", None, "pos", None),
            P(),
            P(),
            P(),
            P(),
            P(),
            P(),
        ),
        check_vma=False,
    )
```

profile of v0, /device:TPU:0, one launch (start us, length us, event | category | flops | bytes accessed | tf_op | source)
XLA Modules:
  0.0 1036.0 jit_solution(2297310748336060298)
XLA Ops:
  18.8 113.3 %all_to_all.63 = bf16[32,64,1152]{2,1,0:T(8,128)(2,1)S(1)} all-to-all(bf16[32,64,1152]{2,1,0:T(8,128)(2,1)S(1)} %bitcast.280), channel_id=1, replica_groups=mesh['pos'=16,'clip'=2] {'pos'}, dimensions={0} | all-to-all | bytes 9437184 | tf_op jit(solution)/shard_map/all_to_all | solution.py:92
  141.2 20.8 %multiply_reduce_fusion.1 = (f32[2,6,1024]{2,1,0:T(8,128)S(1)}, f32[2,6,1024,1024]{2,3,1,0:T(8,128)}) fusion(bf16[2,1024,6,64]{1,3,2,0:T(8,128)(2,1)S(1)} %bitcast.247, bf16[2,1024,6,64]{1,3,2,0:T(8,128)(2,1)} %bitcast.252), kind=kOutput, calls=%fused_computation.6 | convolution fusion | flops 1635766272 | bytes 53526528 | tf_op jit(solution)/shard_map/bqhd,bkhd->bhqk/dot_general | solution.py:63
  162.0 20.1 %fusion = f32[2,6,1024]{2,1,0:T(8,128)S(1)} fusion(f32[2,6,1024,1024]{2,3,1,0:T(8,128)} %get-tuple-element.109, f32[2,6,1024]{2,1,0:T(8,128)S(1)} %get-tuple-element.108), kind=kLoop, calls=%fused_computation.5 | loop fusion | flops 37736448 | bytes 50429952 | tf_op jit(solution)/shard_map/reduce_sum | solution.py:68
  182.1 18.5 %fusion.63 = bf16[2,6,64,1024]{3,2,1,0:T(8,128)(2,1)S(1)} fusion(bf16[2,1024,6,64]{1,3,2,0:T(8,128)(2,1)S(1)} %bitcast.272, f32[2,6,1024,1024]{2,3,1,0:T(8,128)} %get-tuple-element.109, f32[2,6,1024]{2,1,0:T(8,128)S(1)} %fusion, f32[2,6,1024]{2,1,0:T(8,128)S(1)} %get-tuple-element.108), kind=kOutput, calls=%fused_computation.137 | convolution fusion | flops 1661730816 | bytes 53575680 | tf_op jit(solution)/shard_map/bhqk,bkhd->bqhd/dot_general | solution.py:70
  207.6 33.5 %all-to-all-done.1 = bf16[2,1024,384]{2,0,1:T(2,128)(2,1)S(1)} async-done(((bf16[2,1024,384]{2,0,1:T(2,128)(2,1)}), bf16[2,1024,384]{2,0,1:T(2,128)(2,1)S(1)}, u32[]{:S(2)}, u32[]{:S(2)}) %all-to-all-start.1) | async-done | bytes 1572896 | tf_op jit(solution)/shard_map/all_to_all | solution.py:100
  277.4 6.3 reshape.281
  283.7 8.0 multiply_reduce_fusion.3
  305.7 6.2 convert_element_type.128
  322.7 12.8 %fusion.18 = bf16[2,16,64,1536]{3,2,1,0:T(8,128)(2,1)} fusion(f32[2,16,64,1536]{3,2,1,0:T(8,128)S(1)} %fusion.76, bf16[2,1536,384]{2,1,0:T(8,128)(2,1)S(1)} %copy-done.113, bf16[2,16,64,384]{3,2,1,0:T(8,128)(2,1)S(1)} %copy-done.119, f32[2]{0:T(128)S(1)} %multiply_exponential_fusion.1, f32[2,384]{1,0:T(2,128)S(1)} %copy-done.107), kind=kOutput, calls=%fused_computation.27 | convolution fusion | flops 2481979392 | bytes 21630464 | tf_op jit(solution)/shard_map/dot_general | solution.py:54
  343.6 10.4 %multiply_reduce_fusion.4 = (f32[]{:T(128)}, bf16[2,384]{1,0:T(2,128)(2,1)}, bf16[2,16,64,384]{3,2,1,0:T(8,128)(2,1)}, bf16[2,384]{1,0:T(2,128)(2,1)}, f32[2,16,64,384]{3,2,1,0:T(8,128)S(1)}, /*index=5*/f32[]{:T(128)}) fusion(f32[2,384]{1,0:T(2,128)S(1)} %copy-done.107, f32[2]{0:T(128)S(1)} %multiply_exponential_fusion.1, ...), kind=kOutput, calls=%fused_computation.72 | convolution fusion | flops 2461530624 | bytes 29536272 | tf_op jit(solution)/shard_map/dot_general | solution.py:182
  358.0 6.2 reshape.283
  364.2 13.1 %multiply_reduce_fusion.2 = (f32[2,64,6,16]{3,2,1,0:T(8,128)S(1)}, f32[2,64,6,16,16]{3,4,2,1,0:T(8,128)}) fusion(f32[2,64,6,16,16]{3,4,2,1,0:T(8,128)} %copy-done, f32[2,64,6,16]{3,2,1,0:T(8,128)S(1)} %copy-done.31, bf16[2,16,64,6,64]{4,3,2,1,0:T(8,128)(2,1)} %reshape.280, bf16[2,16,64,6,64]{4,3,2,1,0:T(8,128)(2,1)} %reshape.283), kind=kOutput, calls=%fused_computation.33 | convolution fusion | flops 25939968 | bytes 4816896 | tf_op jit(solution)/shard_map/cqphd,ckphd->cphqk/dot_general | solution.py:81
  377.4 6.5 convert_bitcast_fusion
  396.4 6.1 reshape.284
  405.5 6.2 reshape.285
  414.8 6.3 reshape.286
  434.1 12.3 %fusion.11 = bf16[2,16,64,1536]{3,2,1,0:T(8,128)(2,1)} fusion(f32[2,16,64,1536]{3,2,1,0:T(8,128)S(1)} %bitcast.258, bf16[2,1536,384]{2,1,0:T(8,128)(2,1)S(1)} %copy-done.114, f32[2,16,64,384]{3,2,1,0:T(8,128)S(1)} %get-tuple-element.75, f32[2,384]{1,0:T(2,128)S(1)} %get-tuple-element.131), kind=kOutput, calls=%fused_computation.20 | convolution fusion | flops 2480406528 | bytes 23202816 | tf_op jit(solution)/shard_map/dot_general | solution.py:54
  460.8 7.5 all-to-all-start.2
  468.3 33.5 %all-to-all-done.2 = bf16[32,64,384]{2,1,0:T(8,128)(2,1)S(1)} async-done(((bf16[32,64,384]{2,1,0:T(8,128)(2,1)}), bf16[32,64,384]{2,1,0:T(8,128)(2,1)S(1)}, u32[]{:S(2)}, u32[]{:S(2)}) %all-to-all-start.2) | async-done | bytes 1572896 | tf_op jit(solution)/shard_map/all_to_all | solution.py:107
  509.9 19.4 %fusion.60 = bf16[2,6,64,1024]{3,2,1,0:T(8,128)(2,1)} fusion(bf16[2,1024,6,64]{1,3,2,0:T(8,128)(2,1)S(1)} %reshape.288, f32[2,6,1024,1024]{2,3,1,0:T(8,128)} %get-tuple-element.109, f32[2,6,1024]{2,1,0:T(8,128)S(1)} %log_add_fusion.1), kind=kOutput, calls=%fused_computation.134 | convolution fusion | flops 1649147904 | bytes 53526528 | tf_op jit(solution)/shard_map/bhqk,bqhd->bkhd/dot_general | solution.py:122
  529.3 32.2 %multiply_reduce_fusion = (f32[2,6,1024]{2,1,0:T(8,128)S(1)}, f32[2,6,1024,1024]{2,3,1,0:T(8,128)}) fusion(f32[2,6,1024,1024]{2,3,1,0:T(8,128)} %get-tuple-element.109, f32[2,6,1024]{2,1,0:T(8,128)S(1)} %log_add_fusion.1, bf16[2,1024,6,64]{1,3,2,0:T(8,128)(2,1)S(1)} %reshape.288, bf16[2,1024,6,64]{1,3,2,0:T(8,128)(2,1)S(1)} %bitcast.273), kind=kOutput, calls=%fused_computation.1 | convolution fusion | flops 1660932096 | bytes 103907328 | tf_op jit(solution)/shard_map/bqhd,bkhd->bhqk/dot_general | solution.py:81
  561.5 40.1 %multiply_convert_fusion = bf16[2,6,1024,1024]{2,3,1,0:T(8,128)(2,1)} fusion(f32[2,6,1024,1024]{2,3,1,0:T(8,128)} %get-tuple-element.123, f32[2,6,1024,1024]{2,3,1,0:T(8,128)} %get-tuple-element.109, f32[2,6,1024]{2,1,0:T(8,128)S(1)} %get-tuple-element.122, f32[2,6,1024]{2,1,0:T(8,128)S(1)} %log_add_fusion.1), kind=kLoop, calls=%fused_computation | loop fusion | flops 62914560 | bytes 125927424 | tf_op jit(solution)/shard_map/convert_element_type | solution.py:83
  601.5 14.2 %multiply_convert_fusion.6 = bf16[2,6,64,1024]{3,2,1,0:T(8,128)(2,1)} fusion(bf16[2,1024,6,64]{1,3,2,0:T(8,128)(2,1)S(1)} %bitcast.248, bf16[2,6,1024,1024]{2,3,1,0:T(8,128)(2,1)} %multiply_convert_fusion), kind=kOutput, calls=%fused_computation.85 | convolution fusion | flops 1612185600 | bytes 28311552 | tf_op jit(solution)/shard_map/bhqk,bqhd->bkhd/dot_general | solution.py:119
  615.7 13.9 %multiply_convert_fusion.7 = bf16[2,6,64,1024]{3,2,1,0:T(8,128)(2,1)} fusion(bf16[2,1024,6,64]{1,3,2,0:T(8,128)(2,1)S(1)} %bitcast.253, bf16[2,6,1024,1024]{2,3,1,0:T(8,128)(2,1)} %multiply_convert_fusion), kind=kOutput, calls=%fused_computation.86 | convolution fusion | flops 1612185600 | bytes 28311552 | tf_op jit(solution)/shard_map/bhqk,bkhd->bqhd/dot_general | solution.py:84
  640.6 6.7 pad_maximum_fusion
  647.4 7.3 all-to-all-start.3
  661.6 9.9 convolution_bitcast_fusion.1
  692.3 50.1 %all-to-all-done.3 = bf16[2,1024,1152]{2,0,1:T(2,128)(2,1)} async-done(((bf16[2,1024,1152]{2,0,1:T(2,128)(2,1)}), bf16[2,1024,1152]{2,0,1:T(2,128)(2,1)}, u32[]{:S(2)}, u32[]{:S(2)}) %all-to-all-start.3) | async-done | bytes 4718624 | tf_op jit(solution)/shard_map/all_to_all | solution.py:128
  766.9 58.7 %psum.47 = f32[2,3]{1,0:T(2,128)S(1)} all-reduce(f32[2,3]{1,0:T(2,128)S(1)} %pad_maximum_fusion.7), channel_id=1, replica_groups=mesh['pos'=16,'clip'=2] {'pos','clip'}, use_global_device_ids=true, to_apply=%region_45.46 | all-reduce | flops 6 | bytes 48 | tf_op jit(solution)/shard_map/psum | solution.py:305
  825.7 77.1 %psum.42 = bf16[2,2,2304]{2,0,1:T(2,128)(2,1)S(1)} all-reduce(bf16[2,2,2304]{2,0,1:T(2,128)(2,1)S(1)} %pad_maximum_fusion.5), channel_id=1, replica_groups=mesh['pos'=16,'clip'=2] {'pos'}, use_global_device_ids=true, to_apply=%region_34.35 | all-reduce | flops 9216 | bytes 36864 | tf_op jit(solution)/shard_map/psum | solution.py:322
  908.6 8.0 copy.166
  922.5 95.5 %all-reduce.3.cloned.1.call-done = (f32[2,384,1152]{2,1,0:T(8,128)}, f32[2,384,384]{2,1,0:T(8,128)}, f32[2,384,1536]{2,1,0:T(8,128)}, f32[2,1536,384]{2,1,0:T(8,128)}) async-done(((f32[2,384,1152]{2,1,0:T(8,128)}, f32[2,384,384]{2,1,0:T(8,128)}, f32[2,384,1536]{2,1,0:T(8,128)}, f32[2,1536,384]{2,1,0:T(8,128)}), (f32[2,384,1152]{2,1,0:T(8,128)}, f32[2,384,384]{2,1,0:T(8,128)}, f32[2,384,1536]{2,1,0:T(8,128)}, ...) | async-done | bytes 14155792 | tf_op jit(solution)/shard_map/psum | solution.py:336
  (415 shorter events, 239.2 us)
Async XLA Ops:
  14.8 226.7 %copy-start.90 = (f32[2,384]{1,0:T(2,128)}, f32[2,384]{1,0:T(2,128)S(1)}, u32[]{:S(2)}) copy-start(f32[2,384]{1,0:T(2,128)S(1)} %get-tuple-element.126) | copy-start | bytes 9220
  14.8 231.2 %copy-start.73 = (f32[2,384]{1,0:T(2,128)}, f32[2,384]{1,0:T(2,128)S(1)}, u32[]{:S(2)}) copy-start(f32[2,384]{1,0:T(2,128)S(1)} %get-tuple-element.129) | copy-start | bytes 9220
  14.9 231.2 %copy-start.86 = (f32[2,384]{1,0:T(2,128)}, f32[2,384]{1,0:T(2,128)S(1)}, u32[]{:S(2)}) copy-start(f32[2,384]{1,0:T(2,128)S(1)} %get-tuple-element.130) | copy-start | bytes 9220
  14.9 243.3 %copy-start.98 = (f32[2,384]{1,0:T(2,128)}, f32[2,384]{1,0:T(2,128)S(1)}, u32[]{:S(2)}) copy-start(f32[2,384]{1,0:T(2,128)S(1)} %get-tuple-element.97) | copy-start | bytes 9220
  14.9 415.4 %copy-start.84 = (f32[2,384]{1,0:T(2,128)}, f32[2,384]{1,0:T(2,128)S(1)}, u32[]{:S(2)}) copy-start(f32[2,384]{1,0:T(2,128)S(1)} %get-tuple-element.98) | copy-start | bytes 9220
  138.0 24.0 %copy-start.17 = (bf16[2,1024,384]{1,2,0:T(8,128)(2,1)}, bf16[2,1024,384]{1,2,0:T(8,128)(2,1)S(1)}, u32[]{:S(2)}) copy-start(bf16[2,1024,384]{1,2,0:T(8,128)(2,1)S(1)} %copy.133) | copy-start | bytes 4718596
  162.0 20.1 %copy-start.51 = (f32[2,6,1024]{2,1,0:T(8,128)}, f32[2,6,1024]{2,1,0:T(8,128)S(1)}, u32[]{:S(2)}) copy-start(f32[2,6,1024]{2,1,0:T(8,128)S(1)} %get-tuple-element.108) | copy-start | bytes 147460
  162.0 20.1 %copy-start.37 = (bf16[2,1024,384]{1,2,0:T(8,128)(2,1)S(1)}, bf16[2,1024,384]{1,2,0:T(8,128)(2,1)}, u32[]{:S(2)}) copy-start(bf16[2,1024,384]{1,2,0:T(8,128)(2,1)} %copy.132) | copy-start | bytes 4718596
  182.0 18.6 %copy-start.69 = (f32[2,6,1024]{2,1,0:T(8,128)}, f32[2,6,1024]{2,1,0:T(8,128)S(1)}, u32[]{:S(2)}) copy-start(f32[2,6,1024]{2,1,0:T(8,128)S(1)} %fusion) | copy-start | bytes 147460
  203.5 37.7 %all-to-all-start.1 = ((bf16[2,1024,384]{2,0,1:T(2,128)(2,1)}), bf16[2,1024,384]{2,0,1:T(2,128)(2,1)S(1)}, u32[]{:S(2)}, u32[]{:S(2)}) async-start(bf16[2,1024,384]{2,0,1:T(2,128)(2,1)} %copy.136), calls=%async_computation.1 | async-start | bytes 3145728 | tf_op jit(solution)/shard_map/all_to_all | solution.py:100
  207.6 135.9 %copy-start.122 = (f32[2]{0:T(128)}, f32[2]{0:T(128)S(1)}, u32[]{:S(2)}) copy-start(f32[2]{0:T(128)S(1)} %multiply_exponential_fusion.1) | copy-start | bytes 28
  257.4 54.5 %copy-start.4 = (f32[2,16,64,384]{3,2,1,0:T(8,128)}, f32[2,16,64,384]{3,2,1,0:T(8,128)S(1)}, u32[]{:S(2)}) copy-start(f32[2,16,64,384]{3,2,1,0:T(8,128)S(1)} %get-tuple-element.81) | copy-start | bytes 9437188
  257.4 172.8 %copy-start.58 = (f32[2,16,64]{2,1,0:T(8,128)}, f32[2,16,64]{2,1,0:T(8,128)S(1)}, u32[]{:S(2)}) copy-start(f32[2,16,64]{2,1,0:T(8,128)S(1)} %broadcast_multiply_fusion.1) | copy-start | bytes 24580
  258.1 172.2 %copy-start.67 = (f32[2,16,64]{2,1,0:T(8,128)}, f32[2,16,64]{2,1,0:T(8,128)S(1)}, u32[]{:S(2)}) copy-start(f32[2,16,64]{2,1,0:T(8,128)S(1)} %fusion.113) | copy-start | bytes 24580
  316.3 27.2 %copy-start.7 = (f32[2,16,64,384]{3,2,1,0:T(8,128)}, f32[2,16,64,384]{3,2,1,0:T(8,128)S(1)}, u32[]{:S(2)}) copy-start(f32[2,16,64,384]{3,2,1,0:T(8,128)S(1)} %get-tuple-element.79) | copy-start | bytes 9437188
  316.4 27.2 %copy-start.63 = (f32[2,16,64]{2,1,0:T(8,128)}, f32[2,16,64]{2,1,0:T(8,128)S(1)}, u32[]{:S(2)}) copy-start(f32[2,16,64]{2,1,0:T(8,128)S(1)} %broadcast_multiply_fusion) | copy-start | bytes 24580
  317.1 26.5 %copy-start.71 = (f32[2,16,64]{2,1,0:T(8,128)}, f32[2,16,64]{2,1,0:T(8,128)S(1)}, u32[]{:S(2)}) copy-start(f32[2,16,64]{2,1,0:T(8,128)S(1)} %fusion.114) | copy-start | bytes 24580
  322.7 20.9 %copy-start.27 = (f32[2,16,64,1536]{3,2,1,0:T(8,128)}, f32[2,16,64,1536]{3,2,1,0:T(8,128)S(1)}, u32[]{:S(2)}) copy-start(f32[2,16,64,1536]{3,2,1,0:T(8,128)S(1)} %fusion.76) | copy-start | bytes 37748740
  358.0 19.4 %slice-start = ((s8[6291456]{0:T(1024)(128)(4,1)}), s8[2097152]{0:T(1024)(128)(4,1)S(1)}, s32[]{:S(2)}) async-start(s8[6291456]{0:T(1024)(128)(4,1)} %bitcast.245), calls=%async_computation.5 | async-start | bytes 4194304
  433.5 21.0 %copy-start.23 = (f32[2,16,64,384]{3,2,1,0:T(8,128)}, f32[2,16,64,384]{3,2,1,0:T(8,128)S(1)}, u32[]{:S(2)}) copy-start(f32[2,16,64,384]{3,2,1,0:T(8,128)S(1)} %get-tuple-element.75) | copy-start | bytes 9437188
  460.8 41.1 %all-to-all-start.2 = ((bf16[32,64,384]{2,1,0:T(8,128)(2,1)}), bf16[32,64,384]{2,1,0:T(8,128)(2,1)S(1)}, u32[]{:S(2)}, u32[]{:S(2)}) async-start(bf16[32,64,384]{2,1,0:T(8,128)(2,1)} %bitcast.56), calls=%async_computation.2 | async-start | bytes 3145728 | tf_op jit(solution)/shard_map/all_to_all | solution.py:107
  509.9 19.4 %copy-start.38 = (bf16[2,1024,384]{1,2,0:T(8,128)(2,1)S(1)}, bf16[2,1024,384]{1,2,0:T(8,128)(2,1)}, u32[]{:S(2)}) copy-start(bf16[2,1024,384]{1,2,0:T(8,128)(2,1)} %copy.132) | copy-start | bytes 4718596
  561.5 40.1 %copy-start.18 = (bf16[2,1024,384]{1,2,0:T(8,128)(2,1)S(1)}, bf16[2,1024,384]{1,2,0:T(8,128)(2,1)}, u32[]{:S(2)}) copy-start(bf16[2,1024,384]{1,2,0:T(8,128)(2,1)} %copy-done.17) | copy-start | bytes 4718596
  601.5 14.2 %copy-start.19 = (bf16[2,1024,384]{1,2,0:T(8,128)(2,1)S(1)}, bf16[2,1024,384]{1,2,0:T(8,128)(2,1)}, u32[]{:S(2)}) copy-start(bf16[2,1024,384]{1,2,0:T(8,128)(2,1)} %copy.134) | copy-start | bytes 4718596
  647.4 94.9 %all-to-all-start.3 = ((bf16[2,1024,1152]{2,0,1:T(2,128)(2,1)}), bf16[2,1024,1152]{2,0,1:T(2,128)(2,1)}, u32[]{:S(2)}, u32[]{:S(2)}) async-start(bf16[2,1024,1152]{2,0,1:T(2,128)(2,1)} %pad_maximum_fusion), calls=%async_computation.3 | async-start | bytes 9437184 | tf_op jit(solution)/shard_map/all_to_all | solution.py:128
  654.7 363.3 %all-reduce.3.cloned.1.call-start = ((), (), s32[]{:S(2)}) async-start(), calls=%async_computation.4 | async-start | bytes 28311552 | tf_op jit(solution)/shard_map/psum | solution.py:336
  661.6 18.3 %slice-start.10 = ((s8[6291456]{0:T(1024)(128)(4,1)}), s8[4194304]{0:T(1024)(128)(4,1)S(1)}, s32[]{:S(2)}) async-start(s8[6291456]{0:T(1024)(128)(4,1)} %bitcast.265), calls=%async_computation.15 | async-start | bytes 8388608
  661.6 21.8 %slice-start.12 = ((s8[6291456]{0:T(1024)(128)(4,1)}), s8[4194304]{0:T(1024)(128)(4,1)S(1)}, s32[]{:S(2)}) async-start(s8[6291456]{0:T(1024)(128)(4,1)} %bitcast.267), calls=%async_computation.17 | async-start | bytes 8388608
  760.7 64.9 %copy-start.101 = (bf16[2,384]{1,0:T(2,128)(2,1)S(1)}, bf16[2,384]{1,0:T(2,128)(2,1)}, u32[]{:S(2)}) copy-start(bf16[2,384]{1,0:T(2,128)(2,1)} %get-tuple-element.57) | copy-start | bytes 4612
  760.7 64.9 %copy-start.105 = (bf16[2,384]{1,0:T(2,128)(2,1)S(1)}, bf16[2,384]{1,0:T(2,128)(2,1)}, u32[]{:S(2)}) copy-start(bf16[2,384]{1,0:T(2,128)(2,1)} %get-tuple-element.67) | copy-start | bytes 4612
  760.7 64.9 %copy-start.104 = (bf16[2,384]{1,0:T(2,128)(2,1)S(1)}, bf16[2,384]{1,0:T(2,128)(2,1)}, u32[]{:S(2)}) copy-start(bf16[2,384]{1,0:T(2,128)(2,1)} %get-tuple-element.48) | copy-start | bytes 4612
  760.7 64.9 %copy-start.100 = (bf16[2,384]{1,0:T(2,128)(2,1)S(1)}, bf16[2,384]{1,0:T(2,128)(2,1)}, u32[]{:S(2)}) copy-start(bf16[2,384]{1,0:T(2,128)(2,1)} %get-tuple-element.59) | copy-start | bytes 4612
  (114 other events, 555.9 us)
Sparse Core Ops, SparseCore 0:
  751.2 266.8 all-reduce.2
where the time goes:
time: 1040 us
  matrix products  284 us (27%)
  blocking collectives  253 us (24%)
  waiting for transfers between devices  213 us (20%)
  local copies, waits for them, and re-layouts  138 us (13%)
  other arithmetic  113 us (11%)
  starting transfers between devices  19 us (2%)
  between operations  16.1 us (2%)
    all_to_all x1, blocking collectives, spatial_forward(): lax.all_to_all(projected, 'pos', split_axis=0, concat_axis=1, tiled=True)  113 us
    psum x1, waiting for transfers between devices, on_device(): lax.psum((qkv_local, out_local, up_local, down_local), ('pos', 'clip'))  95.5 us
    psum x1, blocking collectives, on_device(): lax.psum(mod_local.astype(jnp.bfloat16), 'pos').astype(jnp.float32)  77.1 us
    psum x1, blocking collectives, on_device(): squares_total = lax.psum(squares_local, ('pos', 'clip'))  58.7 us
    all_to_all x1, waiting for transfers between devices, spatial_backward(): lax.all_to_all(grad_local, 'pos', split_axis=1, concat_axis=0, tiled=True)  50.1 us
    dot_general x8, matrix products, back_dense(): lax.dot_general(grad_rows, weight, (((grad_rows.ndim - 1,), (1,)), ((), (...  50 us
    dot_general x2, matrix products, attend_backward(): jnp.einsum(score_spec, grad_heads, value_heads, preferred_element_type=jn...  45.3 us
    convert_element_type x2, other arithmetic, attend_backward(): grad_scores = (attn_probs * (grad_probs - row_terms)).astype(jnp.bfloat16)  44.7 us
  transfers between devices with their start and end apart: 4, of which 4 were waited for; matrix products, arithmetic and copies ran while one was open for 6% of the time, Pallas kernels for 0%

commit v1 on v0

v1 whole, which is shorter than its diff:
```python
import functools
import math

import jax
import jax.numpy as jnp
from jax import lax
from jax.experimental import pallas as pl
from jax.experimental.pallas import tpu as pltpu
from jax.sharding import PartitionSpec as P

D = 384
HEAD = 64
PAIRS = 3
FF = 1536
EPS = 1e-06
LOG_SCALE = HEAD**-0.5 * math.log2(math.e)
GROUP = 16
FEED_SHAPES = [(D, FF), (FF, D), (D, D)]
VMEM_LIMIT = 56 * 2**20

NN = (((1,), (0,)), ((), ()))
NT = (((1,), (1,)), ((), ()))
TN = (((0,), (0,)), ((), ()))
F32 = jnp.float32
BF = jnp.bfloat16


def mm(left, right, dims=NN):
    return lax.dot_general(left, right, dims, preferred_element_type=F32)


def params():
    return pltpu.CompilerParams(vmem_limit_bytes=VMEM_LIMIT)


def cost(micros):
    return pl.CostEstimate(
        flops=int(micros * 1e9), transcendentals=0, bytes_accessed=int(micros * 3e6)
    )


def norm_rows(values):
    center = values - jnp.mean(values, axis=-1, keepdims=True)
    rstd = lax.rsqrt(jnp.mean(center * center, axis=-1, keepdims=True) + EPS)
    return center * rstd, rstd


def norm_back(grad_normed, normed, rstd):
    mean_grad = jnp.mean(grad_normed, axis=-1, keepdims=True)
    mean_cross = jnp.mean(grad_normed * normed, axis=-1, keepdims=True)
    return rstd * (grad_normed - mean_grad - normed * mean_cross)


def col_sum(values):
    return jnp.sum(values, axis=0, keepdims=True)


def gelu_pair(inner):
    square = inner * inner
    slope = math.sqrt(2.0 / math.pi)
    tanh = jnp.tanh(inner * (slope + (slope * 0.044715) * square))
    half = 0.5 + 0.5 * tanh
    value = inner * half
    grad = half + (value * (1.0 - tanh)) * (slope + (3.0 * 0.044715 * slope) * square)
    return value, grad


def low_lanes():
    return lax.broadcasted_iota(jnp.int32, (1, 2 * HEAD), 1) < HEAD


def both_heads(values, low, fill=0.0):
    other = jnp.full_like(values, fill)
    return (jnp.where(low, values, other), jnp.where(low, other, values))


def whole(shape):
    return pl.BlockSpec(shape, lambda *_: (0,) * len(shape))


def once(shape):
    return pl.BlockSpec(shape, lambda *_: (0,) * len(shape), pipeline_mode=pl.Buffered(1))


def weight_spec(rows, cols, block):
    return pl.BlockSpec((None, rows, cols), lambda *_: (block, 0, 0), pipeline_mode=pl.Buffered(1))


def project_kernel(x_ref, mod_ref, w_ref, out_ref):
    normed, _ = norm_rows(x_ref[...].astype(F32))
    hidden = (normed * (1.0 + mod_ref[1:2]) + mod_ref[0:1]).astype(BF)
    out_ref[...] = mm(hidden, w_ref[...]).astype(BF)


def project(x, mod, qkv_weight, rows):
    n = x.shape[0]
    return pl.pallas_call(
        project_kernel,
        grid=(n // rows,),
        in_specs=[
            pl.BlockSpec((rows, D), lambda i: (i, 0)),
            whole((6, D)),
            weight_spec(D, 3 * D, 0),
        ],
        out_specs=pl.BlockSpec((rows, 3 * D), lambda i: (i, 0)),
        out_shape=jax.ShapeDtypeStruct((n, 3 * D), BF),
        compiler_params=params(),
        cost_estimate=cost(5),
        name="project",
    )(x, mod, qkv_weight)


def attend_kernel(rows, q_ref, k_ref, v_ref, out_ref, log_ref):
    low = low_lanes()
    keys = k_ref[...]
    values = both_heads(v_ref[...], low, 1.0)

    def step(index, carry):
        part = pl.ds(index * rows, rows)
        queries = both_heads(q_ref[part, :], low)
        mixed, tops = [], []
        for head in range(2):
            scores = mm(queries[head], keys, NT)
            top = jnp.max(scores, axis=1, keepdims=True)
            raised = jnp.exp2((scores - top) * LOG_SCALE).astype(BF)
            mixed.append(mm(raised, values[head]))
            tops.append(top * LOG_SCALE)
        total = pltpu.roll(jnp.where(low, mixed[1], mixed[0]), HEAD, 1)
        out_ref[part, :] = (jnp.where(low, mixed[0], mixed[1]) / total).astype(BF)
        log_ref[part, :] = jnp.where(low, tops[0], tops[1]) + jnp.log2(total)
        return carry

    lax.fori_loop(0, q_ref.shape[0] // rows, step, 0)


def attend(qkv, rows):
    n = qkv.shape[0]
    pair = lambda start: pl.BlockSpec((n, 2 * HEAD), lambda p: (0, start + p))
    return pl.pallas_call(
        functools.partial(attend_kernel, rows),
        grid=(PAIRS,),
        in_specs=[pair(0), pair(PAIRS), pair(2 * PAIRS)],
        out_specs=[pair(0), pair(0)],
        out_shape=[jax.ShapeDtypeStruct((n, D), BF), jax.ShapeDtypeStruct((n, D), F32)],
        compiler_params=params(),
        cost_estimate=cost(14),
        name="attend",
    )(qkv, qkv, qkv)


def feed_kernel(
    x_ref,
    att_ref,
    mod_ref,
    wo_ref,
    wu_ref,
    wd_ref,
    next_ref,
    middle_ref,
    branch_ref,
    mlp_ref,
    act_ref,
    slope_ref,
    squares_ref,
):
    @pl.when(pl.program_id(0) == 0)
    def _():
        squares_ref[...] = jnp.zeros_like(squares_ref)

    x = x_ref[...].astype(F32)
    branch = mm(att_ref[...], wo_ref[...])
    gated = mod_ref[2:3] * branch
    middle = x + gated
    normed, _ = norm_rows(middle)
    hidden = (normed * (1.0 + mod_ref[4:5]) + mod_ref[3:4]).astype(BF)
    value, slope = gelu_pair(mm(hidden, wu_ref[...]))
    act = value.astype(BF)
    mlp = mm(act, wd_ref[...])
    fed = mod_ref[5:6] * mlp
    next_ref[...] = (middle + fed).astype(BF)
    middle_ref[...] = middle
    branch_ref[...] = branch.astype(BF)
    mlp_ref[...] = mlp.astype(BF)
    act_ref[...] = act
    slope_ref[...] = slope.astype(BF)
    squares_ref[0:1] += col_sum(x * x)
    squares_ref[1:2] += col_sum(gated * gated)
    squares_ref[2:3] += col_sum(fed * fed)


def feed(x, att, mod, out_weight, up_weight, down_weight, rows):
    n = x.shape[0]
    row = lambda width: pl.BlockSpec((rows, width), lambda i: (i, 0))
    out = lambda width, kind: jax.ShapeDtypeStruct((n, width), kind)
    return pl.pallas_call(
        feed_kernel,
        grid=(n // rows,),
        in_specs=[
            row(D),
            row(D),
            whole((6, D)),
            weight_spec(D, D, 0),
            weight_spec(D, FF, 0),
            weight_spec(FF, D, 0),
        ],
        out_specs=[row(D), row(D), row(D), row(D), row(FF), row(FF), whole((8, D))],
        out_shape=[
            out(D, BF),
            out(D, F32),
            out(D, BF),
            out(D, BF),
            out(FF, BF),
            out(FF, BF),
            jax.ShapeDtypeStruct((8, D), F32),
        ],
        compiler_params=params(),
        cost_estimate=cost(11),
        name="feed",
    )(x, att, mod, out_weight, up_weight, down_weight)


def start_sums(sums, carried):
    for index, total in enumerate(sums):
        total[...] = carried[index][...] if carried else jnp.zeros_like(total)


def row_blocks(total):
    height, width = total.shape
    return [(start, height) for start in range(0, width, D)]


def load_rows(rows_ref, sums):
    at = 0
    for total in sums:
        for start, height in row_blocks(total):
            total[:, start : start + D] = rows_ref[at : at + height]
            at += height


def store_rows(sums, rows_ref):
    at = 0
    for total in sums:
        for start, height in row_blocks(total):
            rows_ref[at : at + height] = total[:, start : start + D].astype(rows_ref.dtype)
            at += height
    if at < rows_ref.shape[0]:
        rows_ref[at:] = jnp.zeros((rows_ref.shape[0] - at, D), rows_ref.dtype)


def split_rows(rows, shapes):
    found, at = [], 0
    for height, width in shapes:
        blocks = []
        for _ in range(width // D):
            blocks.append(rows[at : at + height])
            at += height
        found.append(jnp.concatenate(blocks, axis=1))
    return found


def feed_back_kernel(n_carried, *refs):
    (
        g_ref,
        middle_ref,
        branch_ref,
        mlp_ref,
        act_ref,
        slope_ref,
        att_ref,
        mod_ref,
        wo_ref,
        wu_ref,
        wd_ref,
    ) = refs[:11]
    carried = refs[11 : 11 + n_carried]
    gmid_ref, gatt_ref, part_ref, rows_ref, *sums = refs[11 + n_carried :]

    @pl.when(pl.program_id(0) == 0)
    def _():
        part_ref[...] = jnp.zeros_like(part_ref)
        if carried:
            load_rows(carried[0], sums)
        else:
            start_sums(sums, ())

    up_sum, down_sum, out_sum = sums
    g = g_ref[...].astype(F32)
    part_ref[5:6] += col_sum(mlp_ref[...].astype(F32) * g)
    gm = (mod_ref[5:6] * g).astype(BF)
    down_sum[...] += mm(act_ref[...], gm, TN)
    gi = (slope_ref[...].astype(F32) * mm(gm, wd_ref[...], NT)).astype(BF)
    normed, rstd = norm_rows(middle_ref[...])
    scale = 1.0 + mod_ref[4:5]
    hidden = (normed * scale + mod_ref[3:4]).astype(BF)
    up_sum[...] += mm(hidden, gi, TN)
    gh = mm(gi, wu_ref[...], NT)
    part_ref[3:4] += col_sum(gh)
    part_ref[4:5] += col_sum(gh * normed)
    gmid = g + norm_back(gh * scale, normed, rstd)
    gmid_ref[...] = gmid
    part_ref[2:3] += col_sum(branch_ref[...].astype(F32) * gmid)
    gb = (mod_ref[2:3] * gmid).astype(BF)
    out_sum[...] += mm(att_ref[...], gb, TN)
    gatt_ref[...] = mm(gb, wo_ref[...], NT).astype(BF)

    @pl.when(pl.program_id(0) == pl.num_programs(0) - 1)
    def _():
        store_rows(sums, rows_ref)


def feed_back(g, kept, att, mod, out_weight, up_weight, down_weight, carried, kind, rows, height):
    n = g.shape[0]
    row = lambda width: pl.BlockSpec((rows, width), lambda i: (i, 0))
    shapes = FEED_SHAPES
    return pl.pallas_call(
        functools.partial(feed_back_kernel, len(carried)),
        grid=(n // rows,),
        in_specs=[
            row(D),
            row(D),
            row(D),
            row(D),
            row(FF),
            row(FF),
            row(D),
            whole((6, D)),
            weight_spec(D, D, 0),
            weight_spec(D, FF, 0),
            weight_spec(FF, D, 0),
        ]
        + [once((height, D))] * len(carried),
        out_specs=[row(D), row(D), whole((8, D)), once((height, D))],
        out_shape=[
            jax.ShapeDtypeStruct((n, D), F32),
            jax.ShapeDtypeStruct((n, D), BF),
            jax.ShapeDtypeStruct((8, D), F32),
            jax.ShapeDtypeStruct((height, D), kind),
        ],
        scratch_shapes=[pltpu.VMEM(shape, F32) for shape in shapes],
        compiler_params=params(),
        cost_estimate=cost(16),
        name="feed_back",
    )(g, *kept, att, mod, out_weight, up_weight, down_weight, *carried)


def attend_back_kernel(
    rows, q_ref, k_ref, v_ref, o_ref, log_ref, g_ref, dq_ref, dk_ref, dv_ref, dk_sum, dv_sum
):
    low = low_lanes()
    keys, values = k_ref[...], v_ref[...]
    dk_sum[...] = jnp.zeros_like(dk_sum)
    dv_sum[...] = jnp.zeros_like(dv_sum)

    def step(index, carry):
        part = pl.ds(index * rows, rows)
        queries = both_heads(q_ref[part, :], low)
        grads = both_heads(g_ref[part, :], low)
        cross = both_heads(g_ref[part, :].astype(F32) * o_ref[part, :].astype(F32), low)
        logs = log_ref[part, :]
        found = []
        for head in range(2):
            delta = jnp.sum(cross[head], axis=1, keepdims=True)
            scores = mm(queries[head], keys, NT)
            probs = jnp.exp2(scores * LOG_SCALE - logs[:, HEAD * head : HEAD * head + 1])
            grad_probs = mm(grads[head], values, NT)
            grad_scores = (probs * (grad_probs - delta)).astype(BF)
            found.append(mm(grad_scores, keys))
            dv_sum[...] += mm(grads[head].T, probs.astype(BF))
            dk_sum[...] += mm(queries[head].T, grad_scores)
        dq_ref[part, :] = (jnp.where(low, found[0], found[1]) * HEAD**-0.5).astype(BF)
        return carry

    lax.fori_loop(0, q_ref.shape[0] // rows, step, 0)
    dk_ref[...] = (dk_sum[...] * HEAD**-0.5).T.astype(BF)
    dv_ref[...] = dv_sum[...].T.astype(BF)


def attend_back(qkv, att, logs, grad, rows):
    n = qkv.shape[0]
    pair = lambda start: pl.BlockSpec((n, 2 * HEAD), lambda p: (0, start + p))
    return pl.pallas_call(
        functools.partial(attend_back_kernel, rows),
        grid=(PAIRS,),
        in_specs=[pair(0), pair(PAIRS), pair(2 * PAIRS), pair(0), pair(0), pair(0)],
        out_specs=[pair(0)] * 3,
        out_shape=[jax.ShapeDtypeStruct((n, D), BF)] * 3,
        scratch_shapes=[pltpu.VMEM((2 * HEAD, n), F32)] * 2,
        compiler_params=params(),
        cost_estimate=cost(20),
        name="attend_back",
    )(qkv, qkv, qkv, att, logs, grad)


def project_back_kernel(n_carried, *refs):
    x_ref, dq_ref, dk_ref, dv_ref, gmid_ref, mod_ref, w_ref = refs[:7]
    carried = refs[7 : 7 + n_carried]
    out_ref, part_ref, grad_ref, total = refs[7 + n_carried :]

    @pl.when(pl.program_id(0) == 0)
    def _():
        part_ref[...] = jnp.zeros_like(part_ref)
        if carried:
            load_rows(carried[0], [total])
        else:
            start_sums([total], ())

    normed, rstd = norm_rows(x_ref[...].astype(F32))
    scale = 1.0 + mod_ref[1:2]
    hidden = (normed * scale + mod_ref[0:1]).astype(BF)
    gp = jnp.concatenate([dq_ref[...], dk_ref[...], dv_ref[...]], axis=1)
    total[...] += mm(hidden, gp, TN)
    gh = mm(gp, w_ref[...], NT)
    part_ref[0:1] += col_sum(gh)
    part_ref[1:2] += col_sum(gh * normed)
    out_ref[...] = (gmid_ref[...] + norm_back(gh * scale, normed, rstd)).astype(BF)

    @pl.when(pl.program_id(0) == pl.num_programs(0) - 1)
    def _():
        store_rows([total], grad_ref)


def project_back(x, grads, gmid, mod, qkv_weight, carried, kind, rows):
    n = x.shape[0]
    row = lambda width: pl.BlockSpec((rows, width), lambda i: (i, 0))
    return pl.pallas_call(
        functools.partial(project_back_kernel, len(carried)),
        grid=(n // rows,),
        in_specs=[row(D)] * 5
        + [whole((6, D)), weight_spec(D, 3 * D, 0)]
        + [once((3 * D, D))] * len(carried),
        out_specs=[row(D), whole((8, D)), once((3 * D, D))],
        out_shape=[
            jax.ShapeDtypeStruct((n, D), BF),
            jax.ShapeDtypeStruct((8, D), F32),
            jax.ShapeDtypeStruct((3 * D, D), kind),
        ],
        scratch_shapes=[pltpu.VMEM((D, 3 * D), F32)],
        compiler_params=params(),
        cost_estimate=cost(8),
        name="project_back",
    )(x, *grads, gmid, mod, qkv_weight, *carried)


def temporal_kernel(n_carried, *refs):
    x_ref, cot_ref, code_ref, mod_ref, wq_ref, wo_ref, wu_ref, wd_ref = refs[:8]
    carried = refs[8 : 8 + n_carried]
    refs = refs[8 + n_carried :]
    act_out_ref, g_ref, part_ref = refs[:3]
    out_refs = refs[3:7]
    sums = refs[7:11]
    qkv_ref, att_ref, probs_ref, inv_ref, gatt_ref, gqkv_ref = refs[11:]
    frames, places = x_ref.shape[0], x_ref.shape[1]
    tokens = frames * places
    wide = frames * GROUP
    first = jnp.logical_and(pl.program_id(0) == 0, pl.program_id(1) == 0)
    last = jnp.logical_and(
        pl.program_id(0) == pl.num_programs(0) - 1, pl.program_id(1) == pl.num_programs(1) - 1
    )

    @pl.when(first)
    def _():
        start_sums(sums, carried)

    @pl.when(pl.program_id(1) == 0)
    def _():
        part_ref[...] = jnp.zeros_like(part_ref)

    qkv_sum, out_sum, up_sum, down_sum = sums
    low = low_lanes()
    mod = mod_ref[...]
    x = x_ref[...].reshape(tokens, D).astype(F32)
    normed, rstd = norm_rows(x)
    scale = 1.0 + mod[1:2]
    hidden = (normed * scale + mod[0:1]).astype(BF)
    qkv_ref[...] = mm(hidden, wq_ref[...]).astype(BF).reshape(qkv_ref.shape)

    place = lambda axis: lax.broadcasted_iota(jnp.int32, (wide, wide), axis) % GROUP
    same = place(0) == place(1)
    groups = places // GROUP

    def cut(ref, group, column):
        rows = pl.ds(pl.multiple_of(group * GROUP, GROUP), GROUP)
        return ref[:, rows, column * 2 * HEAD : (column + 1) * 2 * HEAD].reshape(wide, 2 * HEAD)

    def put(ref, group, column, value):
        rows = pl.ds(pl.multiple_of(group * GROUP, GROUP), GROUP)
        ref[:, rows, column * 2 * HEAD : (column + 1) * 2 * HEAD] = value.reshape(
            frames, GROUP, 2 * HEAD
        )

    def attend_group(group, carry):
        for pair in range(PAIRS):
            queries = both_heads(cut(qkv_ref, group, pair), low)
            keys = cut(qkv_ref, group, PAIRS + pair)
            values = both_heads(cut(qkv_ref, group, 2 * PAIRS + pair), low, 1.0)
            mixed = []
            for head in range(2):
                scores = jnp.where(same, mm(queries[head], keys, NT), -1e38)
                top = jnp.max(scores, axis=1, keepdims=True)
                raised = jnp.exp2((scores - top) * LOG_SCALE).astype(BF)
                probs_ref[group * 2 * PAIRS + 2 * pair + head] = raised
                mixed.append(mm(raised, values[head]))
            inverse = 1.0 / pltpu.roll(jnp.where(low, mixed[1], mixed[0]), HEAD, 1)
            put(inv_ref, group, pair, inverse)
            put(att_ref, group, pair, (jnp.where(low, mixed[0], mixed[1]) * inverse).astype(BF))
        return carry

    lax.fori_loop(0, groups, attend_group, 0)

    att = att_ref[...].reshape(tokens, D)
    branch = mm(att, wo_ref[...])
    gated = mod[2:3] * branch
    middle = x + gated
    normed_two, rstd_two = norm_rows(middle)
    scale_two = 1.0 + mod[4:5]
    hidden_two = (normed_two * scale_two + mod[3:4]).astype(BF)
    value, slope = gelu_pair(mm(hidden_two, wu_ref[...]))
    act = value.astype(BF)
    mlp = mm(act, wd_ref[...])
    fed = mod[5:6] * mlp
    act_out_ref[...] = (middle + fed).astype(BF).reshape(act_out_ref.shape)
    part_ref[6:7] += col_sum(x * x)
    part_ref[7:8] += col_sum(gated * gated)
    part_ref[8:9] += col_sum(fed * fed)

    g = cot_ref[...].reshape(tokens, D).astype(F32) * code_ref[0:1]
    part_ref[5:6] += col_sum(mlp * g)
    gm = (mod[5:6] * g).astype(BF)
    down_sum[...] += mm(act, gm, TN)
    gi = (slope * mm(gm, wd_ref[...], NT)).astype(BF)
    up_sum[...] += mm(hidden_two, gi, TN)
    gh = mm(gi, wu_ref[...], NT)
    part_ref[3:4] += col_sum(gh)
    part_ref[4:5] += col_sum(gh * normed_two)
    gmid = g + norm_back(gh * scale_two, normed_two, rstd_two)
    part_ref[2:3] += col_sum(branch * gmid)
    gb = (mod[2:3] * gmid).astype(BF)
    out_sum[...] += mm(att, gb, TN)
    gatt_ref[...] = mm(gb, wo_ref[...], NT).astype(BF).reshape(gatt_ref.shape)

    def back_group(group, carry):
        for pair in range(PAIRS):
            queries = both_heads(cut(qkv_ref, group, pair), low)
            keys = cut(qkv_ref, group, PAIRS + pair)
            values = cut(qkv_ref, group, 2 * PAIRS + pair)
            grad = cut(gatt_ref, group, pair)
            grads = both_heads(grad, low)
            cross = both_heads(grad.astype(F32) * cut(att_ref, group, pair).astype(F32), low)
            inverse = cut(inv_ref, group, pair)
            found = []
            dk = jnp.zeros((wide, 2 * HEAD), F32)
            dv = jnp.zeros((wide, 2 * HEAD), F32)
            for head in range(2):
                delta = jnp.sum(cross[head], axis=1, keepdims=True)
                raised = probs_ref[group * 2 * PAIRS + 2 * pair + head].astype(F32)
                probs = raised * inverse[:, HEAD * head : HEAD * head + 1]
                grad_scores = (probs * (mm(grads[head], values, NT) - delta)).astype(BF)
                found.append(mm(grad_scores, keys))
                dv += mm(probs.astype(BF), grads[head], TN)
                dk += mm(grad_scores, queries[head], TN)
            put(gqkv_ref, group, pair, (jnp.where(low, found[0], found[1]) * HEAD**-0.5).astype(BF))
            put(gqkv_ref, group, PAIRS + pair, (dk * HEAD**-0.5).astype(BF))
            put(gqkv_ref, group, 2 * PAIRS + pair, dv.astype(BF))
        return carry

    lax.fori_loop(0, groups, back_group, 0)

    gp = gqkv_ref[...].reshape(tokens, 3 * D)
    qkv_sum[...] += mm(hidden, gp, TN)
    gh_one = mm(gp, wq_ref[...], NT)
    part_ref[0:1] += col_sum(gh_one)
    part_ref[1:2] += col_sum(gh_one * normed)
    g_next = gmid + norm_back(gh_one * scale, normed, rstd)
    g_ref[...] = g_next.astype(BF).reshape(g_ref.shape)

    @pl.when(last)
    def _():
        for total, out_ref in zip(sums, out_refs):
            out_ref[...] = total[...].astype(out_ref.dtype)


def temporal(x, cot, chunk, codes, mods, weights, carried, kind, places):
    clips, frames, spots, _ = x.shape
    block = lambda offset: pl.BlockSpec(
        (None, frames, places, D), lambda c, p: (offset * clips + c, 0, p, 0)
    )
    per_clip = lambda rows: pl.BlockSpec((None, rows, D), lambda c, p: (chunk * clips + c, 0, 0))
    shapes = [(D, 3 * D), (D, D), (D, FF), (FF, D)]
    kept = lambda width, kind: pltpu.VMEM((frames, places, width), kind)
    groups = places // GROUP
    return pl.pallas_call(
        functools.partial(temporal_kernel, len(carried)),
        grid=(clips, spots // places),
        in_specs=[block(0), block(chunk), per_clip(1), per_clip(6)]
        + [weight_spec(*shape, 1) for shape in shapes]
        + [once(shape) for shape in shapes[: len(carried)]],
        out_specs=[block(0), block(0), pl.BlockSpec((None, 16, D), lambda c, p: (c, 0, 0))]
        + [once(shape) for shape in shapes],
        out_shape=[
            jax.ShapeDtypeStruct(x.shape, BF),
            jax.ShapeDtypeStruct(x.shape, BF),
            jax.ShapeDtypeStruct((clips, 16, D), F32),
        ]
        + [jax.ShapeDtypeStruct(shape, kind) for shape in shapes],
        scratch_shapes=[pltpu.VMEM(shape, F32) for shape in shapes]
        + [
            kept(3 * D, BF),
            kept(D, BF),
            pltpu.VMEM((groups * 2 * PAIRS, frames * GROUP, frames * GROUP), BF),
            kept(D, F32),
            kept(D, BF),
            kept(3 * D, BF),
        ],
        compiler_params=params(),
        cost_estimate=cost(36),
        name="temporal",
    )(x, cot, codes, mods, *weights, *carried)


def embed_steps(timesteps):
    half_width = D // 2
    frequencies = jnp.exp(
        -math.log(10000.0) * jnp.arange(half_width, dtype=F32) / half_width
    )
    angles = timesteps.astype(F32)[:, None] * frequencies[None, :]
    return jax.nn.silu(jnp.concatenate([jnp.cos(angles), jnp.sin(angles)], axis=-1))


def swap(values):
    return lax.all_to_all(values, "pos", split_axis=0, concat_axis=0, tiled=True)


def spread(values, axes, size):
    copies = jnp.broadcast_to(values[None], (size,) + values.shape)
    return lax.all_to_all(copies, axes, split_axis=0, concat_axis=0, tiled=True)


def scatter_rows(rows, n_pos, n_clip):
    me = lax.axis_index("clip")
    part = rows.shape[0] // n_clip
    parts = rows.reshape(n_clip, part, D)
    total = lax.dynamic_index_in_dim(parts, me, 0, keepdims=False).astype(F32)
    for s in range(1, n_clip):
        shift = [(i, (i + s) % n_clip) for i in range(n_clip)]
        give = lax.dynamic_index_in_dim(parts, (me + s) % n_clip, 0, keepdims=False)
        total += lax.ppermute(give, "clip", shift).astype(F32)
    pieces = swap(total.astype(BF).reshape(n_pos, part // n_pos, D))
    return jnp.sum(pieces.astype(F32), axis=0).astype(BF)


def gather_rows(piece, n_pos, n_clip):
    me = lax.axis_index("clip")
    mine = spread(piece, "pos", n_pos)
    if n_clip == 2:
        other = lax.ppermute(mine, "clip", [(0, 1), (1, 0)])
        return jnp.stack([jnp.where(me == 0, mine, other), jnp.where(me == 0, other, mine)])
    full = jnp.zeros((n_clip,) + mine.shape, mine.dtype)
    full = lax.dynamic_update_index_in_dim(full, mine, me, 0)
    for s in range(1, n_clip):
        got = lax.ppermute(mine, "clip", [(i, (i + s) % n_clip) for i in range(n_clip)])
        full = lax.dynamic_update_index_in_dim(full, got, (me - s) % n_clip, 0)
    return full


def round_up(value, unit):
    return -(-value // unit) * unit


def on_device(
    tokens,
    timesteps,
    weight_codes,
    cotangent,
    ada_weight,
    qkv_weight,
    out_weight,
    up_weight,
    down_weight,
):
    clips, frames, spots, _ = tokens.shape
    n_pos = lax.axis_size("pos")
    n_clip = lax.axis_size("clip")
    chunks = clips * frames // n_pos
    span = clips // chunks
    n = n_pos * spots
    rows = 256
    places = min(spots, 32)

    n_all = n_pos * n_clip
    feed_height = round_up(sum(a * b for a, b in FEED_SHAPES) // D, 16 * n_all)
    if feed_height > 4096:
        feed_height = round_up(sum(a * b for a, b in FEED_SHAPES) // D, n_all)

    def send(c):
        return tokens[c * span : (c + 1) * span].reshape(n_pos, spots, D)

    first = swap(send(0))
    embedded = embed_steps(timesteps)
    mods = [
        jnp.dot(
            embedded, ada_weight[block].astype(F32), precision=lax.Precision.HIGHEST
        ).reshape(clips, 6, D)
        for block in range(2)
    ]
    embed_rows = lax.all_gather(embedded, "clip", axis=0, tiled=True)
    scaling = jnp.exp2(0.5 * weight_codes.astype(F32) - 1.0)
    codes = jnp.broadcast_to(scaling[:, None, None], (clips, 1, D))
    mine = lax.axis_index("pos") // frames
    arrived = [first.reshape(n, D)]
    for c in range(1, chunks):
        later, embed_rows, *mods = lax.optimization_barrier((send(c), embed_rows, *mods))
        arrived.append(swap(later).reshape(n, D))

    kept_all = []
    streams = []
    for c in range(chunks):
        x = arrived[c]
        mod = lax.dynamic_index_in_dim(mods[0], c * span + mine, 0, keepdims=False)
        qkv = project(x, mod, qkv_weight, rows)
        att, logs = attend(qkv, 512)
        x_next, *kept, squares = feed(x, att, mod, out_weight, up_weight, down_weight, rows)
        streams.append(swap(x_next.reshape(n_pos, spots, D)).reshape(span, frames, spots, D))
        kept_all.append((x, mod, qkv, att, logs, kept, squares))

    weights = (qkv_weight, out_weight, up_weight, down_weight)
    results, returned, parts_one = [], [], []
    carried = ()
    for c in range(chunks):
        kind = BF if c == chunks - 1 else F32
        result, g, part, *carried = temporal(
            streams[c], cotangent, c, codes, mods[1], weights, carried, kind, places
        )
        results.append(result)
        parts_one.append(part)
        returned.append(swap(g.reshape(n_pos, spots, D)).reshape(n, D))
    sums_one = carried

    axes = ("pos", "clip")
    part_one = jnp.concatenate(parts_one, axis=0)
    squares_zero = sum(kept[-1] for kept in kept_all)[:3]
    squares_one = jnp.sum(part_one[:, 6:9], axis=0)
    squares = jnp.concatenate([squares_zero, squares_one], axis=0)

    def back_of_feed(c, g, carried):
        x, mod, qkv, att, logs, kept, squares = kept_all[c]
        kind = BF if c == chunks - 1 else F32
        weights = (out_weight, up_weight, down_weight)
        return feed_back(g, kept, att, mod, *weights, carried, kind, rows, feed_height)

    def last_block_back(squares, part_one, later, kept_all, middle, carried):
        squares_all = spread(jnp.sum(squares, axis=1).reshape(1, 6), axes, n_all)

        middles = [middle]
        parts_zero = []
        for c in range(1, chunks):
            gmid, gatt, part, *carried = back_of_feed(c, later[c - 1], carried)
            middles.append((gmid, gatt, part))
        feed_piece = scatter_rows(carried[0], n_pos, n_clip)

        carried = ()
        grads = []
        for c in range(chunks):
            kind = BF if c == chunks - 1 else F32
            x, mod, qkv, att, logs, kept, squares = kept_all[c]
            gmid, gatt, part = middles[c]
            found = attend_back(qkv, att, logs, gatt, 256)
            g, part_first, *carried = project_back(
                x, found, gmid, mod, qkv_weight, carried, kind, rows
            )
            grads.append(
                swap(g.reshape(n_pos, spots, D)).reshape(span, frames, spots, D)
            )
            parts_zero.append(part[:6] + part_first[:6])

        own = lax.axis_index("clip") * clips
        mod_all = jnp.zeros((2, n_clip * clips, 6, D), F32)
        for c in range(chunks):
            mod_all = lax.dynamic_update_slice(
                mod_all, parts_zero[c][None, None], (0, own + c * span + mine, 0, 0)
            )
        mod_all = lax.dynamic_update_slice(mod_all, part_one[None, :, :6], (1, own, 0, 0))
        tail = jnp.concatenate([carried[0], mod_all.reshape(-1, D).astype(BF)], axis=0)
        fill = round_up(tail.shape[0], 8 * n_all if n_all <= 32 else n_all) - tail.shape[0]
        tail = jnp.pad(tail, ((0, fill), (0, 0)))
        tail, feed_piece, grads[0] = lax.optimization_barrier((tail, feed_piece, grads[0]))
        piece = jnp.concatenate([feed_piece, scatter_rows(tail, n_pos, n_clip)], axis=0)
        full = gather_rows(piece, n_pos, n_clip)
        feed_rows = feed_piece.shape[0]
        feed_sums = full[:, :, :feed_rows].reshape(-1, D)
        tail = full[:, :, feed_rows:].reshape(-1, D)
        return squares_all, feed_sums, jnp.concatenate(grads, axis=0).astype(F32), tail

    def skip(*operands):
        shapes = jax.eval_shape(last_block_back, *operands)
        return jax.tree.map(lambda leaf: jnp.zeros(leaf.shape, leaf.dtype), shapes)

    gmid, gatt, part, *carried = back_of_feed(0, returned[0], ())
    squares_all, feed_sums, grads, tail = lax.cond(
        timesteps[0] >= 0,
        last_block_back,
        skip,
        squares,
        part_one,
        returned[1:],
        kept_all,
        (gmid, gatt, part),
        carried,
    )
    summed_one = lax.psum(tuple(sums_one), axes)

    n_clips = n_clip * clips
    mod_rows = tail[3 * D : 3 * D + 2 * n_clips * 6].astype(F32).reshape(2, n_clips, 6 * D)
    ada_grad = sum(embed_rows[c][None, :, None] * mod_rows[:, c, None, :] for c in range(n_clips))
    squares_total = jnp.sum(squares_all, axis=(0, 1)).reshape(2, 3)
    stream_rms = jnp.sqrt(squares_total / (clips * frames * spots * n_all))
    up_zero, down_zero, out_zero = split_rows(feed_sums, FEED_SHAPES)
    (qkv_zero,) = split_rows(tail, [(D, 3 * D)])
    stacked = [
        jnp.stack([first.astype(F32), second.astype(F32)])
        for first, second in zip((qkv_zero, out_zero, up_zero, down_zero), summed_one)
    ]
    return (
        jnp.concatenate(results, axis=0),
        grads,
        ada_grad,
        *stacked,
        stream_rms,
    )


def solution(mesh):
    placed = (
        P("clip", None, "pos", None),
        P("clip"),
        P("clip"),
        P("clip", None, "pos", None),
        P(),
        P(),
        P(),
        P(),
        P(),
    )
    return jax.shard_map(
        on_device,
        mesh=mesh,
        in_specs=placed,
        out_specs=(
            P("clip", None, "pos", None),
            P("clip", None, "pos", None),
            P(),
            P(),
            P(),
            P(),
            P(),
            P(),
        ),
        check_vma=False,
    )
```

time: 1040 us -> 499 us (0.48)
  matrix products: 284 us -> 4.51 us
  Pallas kernels: 0 us -> 182 us
  blocking collectives: 253 us -> 88.3 us
  waiting for transfers between devices: 213 us -> 51.2 us
  local copies, waits for them, and re-layouts: 138 us -> 18 us
  starting transfers between devices: 19 us -> 68.2 us
  other arithmetic: 113 us -> 64.1 us
    dot_general x39 -> x2, matrix products: 284 us -> 4.51 us  [on_device(): jnp.dot(embedded, ada_weight[block].astype(F32), precision=lax.Precision....]
    pallas_call x0 -> x13, Pallas kernels: none -> 182 us  [the longest x2 40 us: attend_back(): pl.pallas_call(functools.partial(attend_back_kernel, rows), grid=(PAIRS,)...]
    psum x2 -> x0, blocking collectives: 136 us -> none  [the longest x1 77.1 us: on_device(): lax.psum(mod_local.astype(jnp.bfloat16), 'pos').astype(jnp.float32)]
    psum x1, waiting for transfers between devices: 95.5 us -> 0.01 us  [on_device(): summed_one = lax.psum(tuple(sums_one), axes)]
    all_to_all x3 -> x9, waiting for transfers between devices: 117 us -> 49.3 us  [swap(): lax.all_to_all(values, 'pos', split_axis=0, concat_axis=0, tiled=True)]
    reshape x11 -> x3, local copies, waits for them, and re-layouts: 58.3 us -> 2.79 us  [the longest x1 2.68 us: send(): return tokens[c * span:(c + 1) * span].reshape(n_pos, spots, D)]
    convert_element_type x5 -> x4, other arithmetic: 46.6 us -> 4.6 us  [the longest x1 3 us: last_block_back(): jnp.concatenate(grads, axis=0).astype(F32)]
    all_to_all x3 -> x9, starting transfers between devices: 19 us -> 59.2 us  [swap(): lax.all_to_all(values, 'pos', split_axis=0, concat_axis=0, tiled=True)]
  transfers between devices with their start and end apart: 4 -> 13, of which waited for: 4 -> 6; matrix products, arithmetic and copies ran while one was open for 6% -> 14% of each run, Pallas kernels for 0% -> 37%
where the time goes in v1:
time: 499 us; the launch traced here: 491 us
  Pallas kernels  182 us (36%)
  blocking collectives  88.3 us (18%)
  starting transfers between devices  68.2 us (14%)
  other arithmetic  64.1 us (13%)
  waiting for transfers between devices  51.2 us (10%)
  local copies, waits for them, and re-layouts  18 us (4%)
  between operations  14.9 us (3%)
    all_to_all x9, starting transfers between devices, swap(): lax.all_to_all(values, 'pos', split_axis=0, concat_axis=0, tiled=True)  59.2 us
    all_to_all x2, blocking collectives, spread(): return lax.all_to_all(copies, axes, split_axis=0, concat_axis=0, tiled=True)  59.1 us
    all_to_all x9, waiting for transfers between devices, swap(): lax.all_to_all(values, 'pos', split_axis=0, concat_axis=0, tiled=True)  49.3 us
    pallas_call x2, Pallas kernels, attend_back(): pl.pallas_call(functools.partial(attend_back_kernel, rows), grid=(PAIRS,)...  40 us
    pallas_call x1, other arithmetic, temporal(): pl.pallas_call(functools.partial(temporal_kernel, len(carried)), grid=(cl...  36.3 us
    pallas_call x1, Pallas kernels, temporal(): pl.pallas_call(functools.partial(temporal_kernel, len(carried)), grid=(cl...  35.5 us
    pallas_call x2, Pallas kernels, feed_back(): pl.pallas_call(functools.partial(feed_back_kernel, len(carried)), grid=(n...  32.2 us
    pallas_call x2, Pallas kernels, attend(): pl.pallas_call(functools.partial(attend_kernel, rows), grid=(PAIRS,), in_...  28.6 us
  transfers between devices with their start and end apart: 13, of which 6 were waited for; matrix products, arithmetic and copies ran while one was open for 14% of the time, Pallas kernels for 37%

profile of v1, /device:TPU:0, one launch (start us, length us, event | category | flops | bytes accessed | tf_op | source)
XLA Modules:
  0.0 491.1 jit_solution(6330634500021331803)
XLA Ops:
  9.9 8.4 %all-to-all-start.6 = ((bf16[16,64,384]{2,1,0:T(8,128)(2,1)}), bf16[16,64,384]{2,1,0:T(8,128)(2,1)}, u32[]{:S(2)}, u32[]{:S(2)}) async-start(bf16[16,64,384]{2,1,0:T(8,128)(2,1)} %get-tuple-element.230), calls=%async_computation.6 | async-start | bytes 1572864 | tf_op jit(solution)/shard_map/all_to_all | solution.py:630
  31.0 7.0 %all-to-all-done.6 = bf16[16,64,384]{2,1,0:T(8,128)(2,1)} async-done(((bf16[16,64,384]{2,1,0:T(8,128)(2,1)}), bf16[16,64,384]{2,1,0:T(8,128)(2,1)}, u32[]{:S(2)}, u32[]{:S(2)}) %all-to-all-start.6) | async-done | bytes 786464 | tf_op jit(solution)/shard_map/all_to_all | solution.py:630
  38.0 4.9 all-to-all-start.8
  42.9 5.3 %project.2.q_ref.k_ref.v_ref = bf16[1024,1152]{1,0:T(8,128)(2,1)} custom-call(bf16[1024,384]{1,0:T(8,128)(2,1)} %bitcast.21.x_ref, f32[6,384]{1,0:T(8,128)S(1)} %bitcast.125, bf16[2,384,1152]{2,1,0:T(8,128)(2,1)} %w_ref.3), custom_call_target="tpu_custom_call" | custom-call | flops 5000000000 | bytes 15000000 | tf_op jit(solution)/shard_map/project/pallas_call | solution.py:97
  48.3 14.3 %attend.2 = (bf16[1024,384]{1,0:T(8,128)(2,1)S(1)}, f32[1024,384]{1,0:T(8,128)}) custom-call(bf16[1024,1152]{1,0:T(8,128)(2,1)} %project.2.q_ref.k_ref.v_ref, bf16[1024,1152]{1,0:T(8,128)(2,1)} %project.2.q_ref.k_ref.v_ref, bf16[1024,1152]{1,0:T(8,128)(2,1)} %project.2.q_ref.k_ref.v_ref), custom_call_target="tpu_custom_call" | custom-call | flops 14000000000 | bytes 42000000 | tf_op jit(solution)/shard_map/attend/pallas_call | solution.py:139
  63.5 9.8 %feed.2 = (bf16[1024,384]{1,0:T(8,128)(2,1)}, f32[1024,384]{1,0:T(8,128)}, bf16[1024,384]{1,0:T(8,128)(2,1)}, bf16[1024,384]{1,0:T(8,128)(2,1)}, bf16[1024,1536]...) custom-call(bf16[1024,384]{1,0:T(8,128)(2,1)} %bitcast.21.x_ref, ...), custom_call_target="tpu_custom_call" | custom-call | flops 11000000512 | bytes 33000000 | tf_op jit(solution)/shard_map/feed/pallas_call | solution.py:195
  73.3 7.2 %all-to-all-start.7 = ((bf16[16,64,384]{2,1,0:T(8,128)(2,1)}), bf16[16,64,384]{2,1,0:T(8,128)(2,1)S(1)}, u32[]{:S(2)}, u32[]{:S(2)}) async-start(bf16[16,64,384]{2,1,0:T(8,128)(2,1)} %bitcast.122), calls=%async_computation.7 | async-start | bytes 1572864 | tf_op jit(solution)/shard_map/all_to_all | solution.py:630
  80.4 4.9 project.3.q_ref.k_ref.v_ref
  85.3 14.3 %attend.3 = (bf16[1024,384]{1,0:T(8,128)(2,1)S(1)}, f32[1024,384]{1,0:T(8,128)}) custom-call(bf16[1024,1152]{1,0:T(8,128)(2,1)} %project.3.q_ref.k_ref.v_ref, bf16[1024,1152]{1,0:T(8,128)(2,1)} %project.3.q_ref.k_ref.v_ref, bf16[1024,1152]{1,0:T(8,128)(2,1)} %project.3.q_ref.k_ref.v_ref), custom_call_target="tpu_custom_call" | custom-call | flops 14000000000 | bytes 42000000 | tf_op jit(solution)/shard_map/attend/pallas_call | solution.py:139
  99.7 8.9 %feed.3 = (bf16[1024,384]{1,0:T(8,128)(2,1)}, f32[1024,384]{1,0:T(8,128)}, bf16[1024,384]{1,0:T(8,128)(2,1)}, bf16[1024,384]{1,0:T(8,128)(2,1)}, bf16[1024,1536]...) custom-call(bf16[1024,384]{1,0:T(8,128)(2,1)S(1)} %bitcast.114, ...), custom_call_target="tpu_custom_call" | custom-call | flops 11000000512 | bytes 33000000 | tf_op jit(solution)/shard_map/feed/pallas_call | solution.py:195
  108.6 7.0 %all-to-all-start.9 = ((bf16[16,64,384]{2,1,0:T(8,128)(2,1)}), bf16[16,64,384]{2,1,0:T(8,128)(2,1)S(1)}, u32[]{:S(2)}, u32[]{:S(2)}) async-start(bf16[16,64,384]{2,1,0:T(8,128)(2,1)} %bitcast.123), calls=%async_computation.9 | async-start | bytes 1572864 | tf_op jit(solution)/shard_map/all_to_all | solution.py:630
  116.3 35.5 %temporal.2 = (bf16[1,16,64,384]{3,2,1,0:T(8,128)(2,1)}, bf16[1,16,64,384]{3,2,1,0:T(8,128)(2,1)}, f32[1,16,384]{2,1,0:T(8,128)}, f32[384,1152]{1,0:T(8,128)}, f...) custom-call(bf16[1,16,64,384]{3,2,1,0:T(8,128)(2,1)} %bitcast.121, bf16[2,16,64,384]{3,2,1,0:T(8,128)(2,1)} %refs_1_.2, ...), custom_call_target="tpu_custom_call" | custom-call | flops 35999997952 | bytes 108000000 | tf_op jit(solution)/shard_map/temporal/pallas_call | solution.py:591
  151.8 6.9 %all-to-all-start.11 = ((bf16[16,64,384]{2,1,0:T(8,128)(2,1)}), bf16[16,64,384]{2,1,0:T(8,128)(2,1)S(1)}, u32[]{:S(2)}, u32[]{:S(2)}) async-start(bf16[16,64,384]{2,1,0:T(8,128)(2,1)} %bitcast.119), calls=%async_computation.11 | async-start | bytes 1572864 | tf_op jit(solution)/shard_map/all_to_all | solution.py:630
  158.8 8.8 %all-reduce.4.cloned.1.call-start = ((), (), s32[]{:S(2)}) async-start(), calls=%async_computation.12 | async-start | bytes 7077888 | tf_op jit(solution)/shard_map/psum | solution.py:809
  168.4 36.3 %temporal.3 = (f32[2,16,384]{2,1,0:T(8,128)S(1)}, bf16[1,16,64,384]{3,2,1,0:T(8,128)(2,1)S(1)}, bf16[1,16,64,384]{3,2,1,0:T(8,128)(2,1)}, bf16[384,1152]{1,0:T(8...) fusion(f32[2,16,384]{2,1,0:T(8,128)S(1)} %constant_dynamic-update-slice_fusion.1, ...), kind=kCustom, calls=%fused_computation.50 | custom fusion | flops 35999997952 | bytes 21679104 | tf_op jit(solution)/shard_map/temporal/pallas_call | solution.py:591
  207.2 6.9 %all-to-all-start.10 = ((bf16[16,64,384]{2,1,0:T(8,128)(2,1)}), bf16[16,64,384]{2,1,0:T(8,128)(2,1)S(1)}, u32[]{:S(2)}, u32[]{:S(2)}) async-start(bf16[16,64,384]{2,1,0:T(8,128)(2,1)} %bitcast.37), calls=%async_computation.10 | async-start | bytes 1572864 | tf_op jit(solution)/shard_map/all_to_all | solution.py:630
  214.1 15.7 %feed_back.3 = (f32[1024,384]{1,0:T(8,128)}, bf16[1024,384]{1,0:T(8,128)(2,1)}, f32[8,384]{1,0:T(8,128)S(1)}, f32[3584,384]{1,0:T(8,128)}) custom-call(bf16[1024,384]{1,0:T(8,128)(2,1)} %bitcast.117, f32[1024,384]{1,0:T(8,128)} %get-tuple-element.174.refs_1_, bf16[1024,384]{1,0:T(8,128)(2,1)} %get-tuple-element.175.refs_2_, ...), custom_call_target="tpu_custom_call" | custom-call | flops 16000000000 | bytes 48000000 | tf_op jit(solution)/shard_map/feed_back/pallas_call | solution.py:315
  229.9 8.6 %all-to-all-done.10 = bf16[16,64,384]{2,1,0:T(8,128)(2,1)S(1)} async-done(((bf16[16,64,384]{2,1,0:T(8,128)(2,1)}), bf16[16,64,384]{2,1,0:T(8,128)(2,1)S(1)}, u32[]{:S(2)}, u32[]{:S(2)}) %all-to-all-start.10) | async-done | bytes 786464 | tf_op jit(solution)/shard_map/all_to_all | solution.py:630
  238.4 225.8 %conditional.1 = (bf16[3584,384]{1,0:T(8,128)(2,1)S(1)}, f32[2,16,64,384]{3,2,1,0:T(8,128)}, bf16[1280,384]{1,0:T(8,128)(2,1)}, f32[2,3]{1,0:T(2,128)S(1)}) conditional(s32[]{:T(128)} %bitcast.36, () %tuple.21, (bf16[16,64,384]{2,1,0:T(8,128)(2,1)S(1)}, f32[1024,384]{1,0:T(8,128)}, bf16[1024,384]{1,0:T(8,128)(2,1)}, bf16[1024,384]{1,0:T(8,128)(2,1)}, ...), branch_computations={%region_1.2_spmd, %region_2.7_spmd} | conditional | flops 72015069184 | bytes 319843872 | solution.py:798
  238.4 16.5 %feed_back.2 = (f32[1024,384]{1,0:T(8,128)}, bf16[1024,384]{1,0:T(8,128)(2,1)}, f32[8,384]{1,0:T(8,128)}, bf16[3584,384]{1,0:T(8,128)(2,1)}) custom-call(bf16[1024,384]{1,0:T(8,128)(2,1)S(1)} %bitcast.116, f32[1024,384]{1,0:T(8,128)} %get-tuple-element.61.refs_1_, bf16[1024,384]{1,0:T(8,128)(2,1)} %get-tuple-element.62.refs_2_, ...), custom_call_target="tpu_custom_call" | custom-call | flops 16000000000 | bytes 48000000 | tf_op jit(solution)/shard_map/cond/branch_1_fun/feed_back/pallas_call | solution.py:315
  256.6 20.1 %attend_back.3 = (bf16[1024,384]{1,0:T(8,128)(2,1)}, bf16[1024,384]{1,0:T(8,128)(2,1)}, bf16[1024,384]{1,0:T(8,128)(2,1)}) custom-call(bf16[1024,1152]{1,0:T(8,128)(2,1)} %get-tuple-element.78.q_ref.k_ref.v_ref, bf16[1024,1152]{1,0:T(8,128)(2,1)} %get-tuple-element.78.q_ref.k_ref.v_ref, bf16[1024,1152]{1,0:T(8,128)(2,1)} %get-tuple-element.78.q_ref.k_ref.v_ref, ...), custom_call_target="tpu_custom_call" | custom-call | flops 20000000000 | bytes 60000000 | tf_op jit(solution)/shard_map/cond/branch_1_fun/attend_back/pallas_call | solution.py:381
  278.3 6.2 %all-to-all-start = ((bf16[16,112,384]{2,1,0:T(8,128)(2,1)}), bf16[16,112,384]{2,1,0:T(8,128)(2,1)S(1)}, u32[]{:S(2)}, u32[]{:S(2)}) async-start(bf16[16,112,384]{2,1,0:T(8,128)(2,1)} %bitcast.7), calls=%async_computation | async-start | bytes 2752512 | tf_op jit(solution)/shard_map/cond/branch_1_fun/all_to_all | solution.py:630
  284.5 8.2 %project_back.2 = (bf16[1024,384]{1,0:T(8,128)(2,1)}, f32[8,384]{1,0:T(8,128)}, f32[1152,384]{1,0:T(8,128)}) custom-call(bf16[1024,384]{1,0:T(8,128)(2,1)} %get-tuple-element.77.refs_0_, bf16[1024,384]{1,0:T(8,128)(2,1)} %get-tuple-element.82.refs_1_, bf16[1024,384]{1,0:T(8,128)(2,1)} %get-tuple-element.83.refs_2_, ...), custom_call_target="tpu_custom_call" | custom-call | flops 8000000000 | bytes 24000000 | tf_op jit(solution)/shard_map/cond/branch_1_fun/project_back/pallas_call | solution.py:425
  292.8 19.9 %attend_back.2 = (bf16[1024,384]{1,0:T(8,128)(2,1)}, bf16[1024,384]{1,0:T(8,128)(2,1)}, bf16[1024,384]{1,0:T(8,128)(2,1)}) custom-call(bf16[1024,1152]{1,0:T(8,128)(2,1)S(1)} %copy-done.30, bf16[1024,1152]{1,0:T(8,128)(2,1)S(1)} %copy-done.30, bf16[1024,1152]{1,0:T(8,128)(2,1)S(1)} %copy-done.30, bf16[1024,384]{1,0:T(8,128)(2,1)S(1)} %copy-done.34, ...), custom_call_target="tpu_custom_call" | custom-call | flops 20000000000 | bytes 60000000 | tf_op jit(solution)/shard_map/cond/branch_1_fun/attend_back/pallas_call | solution.py:381
  312.7 4.6 all-to-all-done
  317.2 7.5 %all-to-all-start.1 = ((bf16[16,64,384]{2,1,0:T(8,128)(2,1)}), bf16[16,64,384]{2,1,0:T(8,128)(2,1)S(1)}, u32[]{:S(2)}, u32[]{:S(2)}) async-start(bf16[16,64,384]{2,1,0:T(8,128)(2,1)} %bitcast.118), calls=%async_computation.1 | async-start | bytes 1572864 | tf_op jit(solution)/shard_map/cond/branch_1_fun/all_to_all | solution.py:630
  324.8 8.2 %project_back.3 = (bf16[1024,384]{1,0:T(8,128)(2,1)}, f32[8,384]{1,0:T(8,128)}, bf16[1152,384]{1,0:T(8,128)(2,1)}) custom-call(bf16[1024,384]{1,0:T(8,128)(2,1)S(1)} %copy-done.11, bf16[1024,384]{1,0:T(8,128)(2,1)} %get-tuple-element.72.refs_1_, bf16[1024,384]{1,0:T(8,128)(2,1)} %get-tuple-element.73.refs_2_, bf16[1024,384]{1,0:T(8,128)(2,1)} %get-tuple-element.74.refs_3_, ...), custom_call_target="tpu_custom_call" | custom-call | flops 8000000000 | bytes 24000000 | tf_op jit(solution)/shard_map/cond/branch_1_fun/project_back/pallas_call | solution.py:425
  335.2 9.2 %all-to-all-done.1 = bf16[16,64,384]{2,1,0:T(8,128)(2,1)S(1)} async-done(((bf16[16,64,384]{2,1,0:T(8,128)(2,1)}), bf16[16,64,384]{2,1,0:T(8,128)(2,1)S(1)}, u32[]{:S(2)}, u32[]{:S(2)}) %all-to-all-start.1) | async-done | bytes 786464 | tf_op jit(solution)/shard_map/cond/branch_1_fun/all_to_all | solution.py:630
  346.5 27.3 %all_to_all.54 = bf16[16,40,384]{2,1,0:T(8,128)(2,1)S(1)} all-to-all(bf16[16,40,384]{2,1,0:T(8,128)(2,1)S(1)} %bitcast.109), channel_id=1, replica_groups=mesh['pos'=16,'clip'=2] {'pos'}, dimensions={0} | all-to-all | bytes 983040 | tf_op jit(solution)/shard_map/cond/branch_1_fun/all_to_all | solution.py:630
  374.1 49.6 %all_to_all.55 = bf16[16,152,384]{2,1,0:T(8,128)(2,1)S(1)} all-to-all(bf16[16,152,384]{2,1,0:T(8,128)(2,1)S(1)} %broadcast_in_dim.3), channel_id=1, replica_groups=mesh['pos'=16,'clip'=2] {'pos'}, dimensions={0} | all-to-all | bytes 3735552 | tf_op jit(solution)/shard_map/cond/branch_1_fun/all_to_all | solution.py:635
  423.9 9.5 %all_to_all.56 = f32[32,1,6]{2,1,0:T(1,128)S(1)} all-to-all(f32[32,1,6]{2,1,0:T(1,128)S(1)} %broadcast_in_dim.4), channel_id=1, replica_groups=mesh['pos'=16,'clip'=2] {'pos','clip'}, dimensions={0} | all-to-all | bytes 1536 | tf_op jit(solution)/shard_map/cond/branch_1_fun/all_to_all | solution.py:635
  437.8 19.9 %all-to-all-done.4 = bf16[16,64,384]{2,1,0:T(8,128)(2,1)} async-done(((bf16[16,64,384]{2,1,0:T(8,128)(2,1)}), bf16[16,64,384]{2,1,0:T(8,128)(2,1)}, u32[]{:S(2)}, u32[]{:S(2)}) %all-to-all-start.4) | async-done | bytes 786464 | tf_op jit(solution)/shard_map/cond/branch_1_fun/all_to_all | solution.py:630
  (142 shorter events, 58.3 us)
Async XLA Ops:
  7.2 11.1 %copy-start.28 = (s32[2]{0:T(128)S(1)}, s32[2]{0:T(128)}, u32[]{:S(2)}) copy-start(s32[2]{0:T(128)} %param.12) | copy-start | bytes 28
  9.9 28.2 %all-to-all-start.6 = ((bf16[16,64,384]{2,1,0:T(8,128)(2,1)}), bf16[16,64,384]{2,1,0:T(8,128)(2,1)}, u32[]{:S(2)}, u32[]{:S(2)}) async-start(bf16[16,64,384]{2,1,0:T(8,128)(2,1)} %get-tuple-element.230), calls=%async_computation.6 | async-start | bytes 1572864 | tf_op jit(solution)/shard_map/all_to_all | solution.py:630
  38.0 35.2 %all-to-all-start.8 = ((bf16[16,64,384]{2,1,0:T(8,128)(2,1)}), bf16[16,64,384]{2,1,0:T(8,128)(2,1)S(1)}, u32[]{:S(2)}, u32[]{:S(2)}) async-start(bf16[16,64,384]{2,1,0:T(8,128)(2,1)} %get-tuple-element.159), calls=%async_computation.8 | async-start | bytes 1572864 | tf_op jit(solution)/shard_map/all_to_all | solution.py:630
  48.3 15.2 %copy-start.21 = (bf16[2,384,1536]{2,1,0:T(8,128)(2,1)S(1)}, bf16[2,384,1536]{2,1,0:T(8,128)(2,1)}, u32[]{:S(2)}) copy-start(bf16[2,384,1536]{2,1,0:T(8,128)(2,1)} %refs_9_.1) | copy-start | bytes 7077892
  48.3 15.2 %copy-start.23 = (bf16[2,1536,384]{2,1,0:T(8,128)(2,1)S(1)}, bf16[2,1536,384]{2,1,0:T(8,128)(2,1)}, u32[]{:S(2)}) copy-start(bf16[2,1536,384]{2,1,0:T(8,128)(2,1)} %refs_10_.1) | copy-start | bytes 7077892
  48.3 15.2 %copy-start.25 = (bf16[2,384,384]{2,1,0:T(8,128)(2,1)S(1)}, bf16[2,384,384]{2,1,0:T(8,128)(2,1)}, u32[]{:S(2)}) copy-start(bf16[2,384,384]{2,1,0:T(8,128)(2,1)} %refs_8_.1) | copy-start | bytes 1769476
  73.3 35.3 %all-to-all-start.7 = ((bf16[16,64,384]{2,1,0:T(8,128)(2,1)}), bf16[16,64,384]{2,1,0:T(8,128)(2,1)S(1)}, u32[]{:S(2)}, u32[]{:S(2)}) async-start(bf16[16,64,384]{2,1,0:T(8,128)(2,1)} %bitcast.122), calls=%async_computation.7 | async-start | bytes 1572864 | tf_op jit(solution)/shard_map/all_to_all | solution.py:630
  85.3 14.3 %copy-start.22 = (bf16[2,384,1536]{2,1,0:T(8,128)(2,1)S(1)}, bf16[2,384,1536]{2,1,0:T(8,128)(2,1)}, u32[]{:S(2)}) copy-start(bf16[2,384,1536]{2,1,0:T(8,128)(2,1)} %refs_9_.1) | copy-start | bytes 7077892
  85.3 14.3 %copy-start.24 = (bf16[2,1536,384]{2,1,0:T(8,128)(2,1)S(1)}, bf16[2,1536,384]{2,1,0:T(8,128)(2,1)}, u32[]{:S(2)}) copy-start(bf16[2,1536,384]{2,1,0:T(8,128)(2,1)} %refs_10_.1) | copy-start | bytes 7077892
  85.3 14.3 %copy-start.26 = (bf16[2,384,384]{2,1,0:T(8,128)(2,1)S(1)}, bf16[2,384,384]{2,1,0:T(8,128)(2,1)}, u32[]{:S(2)}) copy-start(bf16[2,384,384]{2,1,0:T(8,128)(2,1)} %refs_8_.1) | copy-start | bytes 1769476
  99.7 8.9 %copy-start.33 = (bf16[1024,384]{1,0:T(8,128)(2,1)}, bf16[1024,384]{1,0:T(8,128)(2,1)S(1)}, u32[]{:S(2)}) copy-start(bf16[1024,384]{1,0:T(8,128)(2,1)S(1)} %get-tuple-element.160.att_ref) | copy-start | bytes 2359300
  108.6 43.2 %all-to-all-start.9 = ((bf16[16,64,384]{2,1,0:T(8,128)(2,1)}), bf16[16,64,384]{2,1,0:T(8,128)(2,1)S(1)}, u32[]{:S(2)}, u32[]{:S(2)}) async-start(bf16[16,64,384]{2,1,0:T(8,128)(2,1)} %bitcast.123), calls=%async_computation.9 | async-start | bytes 1572864 | tf_op jit(solution)/shard_map/all_to_all | solution.py:630
  116.3 51.3 %copy-start.29 = (s32[2]{0:T(128)S(1)}, s32[2]{0:T(128)}, u32[]{:S(2)}) copy-start(s32[2]{0:T(128)} %param.12) | copy-start | bytes 28
  116.3 51.3 %copy-start.19 = (f32[8,384]{1,0:T(8,128)S(1)}, f32[8,384]{1,0:T(8,128)}, u32[]{:S(2)}) copy-start(f32[8,384]{1,0:T(8,128)} %get-tuple-element.187) | copy-start | bytes 36868
  116.3 51.3 %copy-start.20 = (f32[8,384]{1,0:T(8,128)S(1)}, f32[8,384]{1,0:T(8,128)}, u32[]{:S(2)}) copy-start(f32[8,384]{1,0:T(8,128)} %get-tuple-element.188) | copy-start | bytes 36868
  116.3 52.1 %copy-start.15 = (f32[2,6,384]{2,1,0:T(8,128)S(1)}, f32[2,6,384]{2,1,0:T(8,128)}, u32[]{:S(2)}) copy-start(f32[2,6,384]{2,1,0:T(8,128)} %copy.61.refs_3_) | copy-start | bytes 55300
  116.3 52.1 %copy-start.18 = (f32[2,1,384]{2,1,0:T(1,128)S(1)}, f32[2,1,384]{2,1,0:T(1,128)}, u32[]{:S(2)}) copy-start(f32[2,1,384]{2,1,0:T(1,128)} %broadcast_in_dim.12.refs_2_) | copy-start | bytes 9220
  151.8 55.4 %all-to-all-start.11 = ((bf16[16,64,384]{2,1,0:T(8,128)(2,1)}), bf16[16,64,384]{2,1,0:T(8,128)(2,1)S(1)}, u32[]{:S(2)}, u32[]{:S(2)}) async-start(bf16[16,64,384]{2,1,0:T(8,128)(2,1)} %bitcast.119), calls=%async_computation.11 | async-start | bytes 1572864 | tf_op jit(solution)/shard_map/all_to_all | solution.py:630
  158.8 314.4 %all-reduce.4.cloned.1.call-start = ((), (), s32[]{:S(2)}) async-start(), calls=%async_computation.12 | async-start | bytes 7077888 | tf_op jit(solution)/shard_map/psum | solution.py:809
  207.2 31.2 %all-to-all-start.10 = ((bf16[16,64,384]{2,1,0:T(8,128)(2,1)}), bf16[16,64,384]{2,1,0:T(8,128)(2,1)S(1)}, u32[]{:S(2)}, u32[]{:S(2)}) async-start(bf16[16,64,384]{2,1,0:T(8,128)(2,1)} %bitcast.37), calls=%async_computation.10 | async-start | bytes 1572864 | tf_op jit(solution)/shard_map/all_to_all | solution.py:630
  238.4 16.5 %copy-start.10 = (bf16[1024,384]{1,0:T(8,128)(2,1)}, bf16[1024,384]{1,0:T(8,128)(2,1)S(1)}, u32[]{:S(2)}) copy-start(bf16[1024,384]{1,0:T(8,128)(2,1)S(1)} %get-tuple-element.56.refs_0_) | copy-start | bytes 2359300 | tf_op jit(solution)/shard_map/cond
  256.5 20.2 %collective-permute-start = (bf16[1792,384]{1,0:T(8,128)(2,1)S(1)}, bf16[1792,384]{1,0:T(8,128)(2,1)S(1)}, u32[]{:S(2)}, u32[]{:S(2)}) collective-permute-start(bf16[1792,384]{1,0:T(8,128)(2,1)S(1)} %dynamic-slice_bitcast_fusion), channel_id=1, source_target_pairs={{0,1},{1,0},{2,3},{3,2},{4,5},{5,4},{6,7},{7,6},{8,9},{9,8},{10,11... | collective-permute-start | bytes 4128776 | tf_op jit(solution)/shard_map/cond/branch_1_fun/ppermute | solution.py:646
  256.6 20.2 %copy-start.1 = (bf16[3584,384]{1,0:T(8,128)(2,1)S(1)}, bf16[3584,384]{1,0:T(8,128)(2,1)}, u32[]{:S(2)}) copy-start(bf16[3584,384]{1,0:T(8,128)(2,1)} %get-tuple-element.95) | copy-start | bytes 8257540 | tf_op jit(solution)/shard_map/cond
  278.3 39.0 %all-to-all-start = ((bf16[16,112,384]{2,1,0:T(8,128)(2,1)}), bf16[16,112,384]{2,1,0:T(8,128)(2,1)S(1)}, u32[]{:S(2)}, u32[]{:S(2)}) async-start(bf16[16,112,384]{2,1,0:T(8,128)(2,1)} %bitcast.7), calls=%async_computation | async-start | bytes 2752512 | tf_op jit(solution)/shard_map/cond/branch_1_fun/all_to_all | solution.py:630
  284.4 8.3 %copy-start.30 = (bf16[1024,1152]{1,0:T(8,128)(2,1)S(1)}, bf16[1024,1152]{1,0:T(8,128)(2,1)}, u32[]{:S(2)}) copy-start(bf16[1024,1152]{1,0:T(8,128)(2,1)} %get-tuple-element.57.q_ref.k_ref.v_ref) | copy-start | bytes 7077892 | tf_op jit(solution)/shard_map/cond
  284.5 8.3 %copy-start.31 = (f32[1024,384]{1,0:T(8,128)S(1)}, f32[1024,384]{1,0:T(8,128)}, u32[]{:S(2)}) copy-start(f32[1024,384]{1,0:T(8,128)} %get-tuple-element.59.log_ref) | copy-start | bytes 4718596 | tf_op jit(solution)/shard_map/cond
  292.7 32.0 %copy-start.17 = (f32[8,384]{1,0:T(8,128)S(1)}, f32[8,384]{1,0:T(8,128)}, u32[]{:S(2)}) copy-start(f32[8,384]{1,0:T(8,128)} %get-tuple-element.90) | copy-start | bytes 36868 | tf_op jit(solution)/shard_map/cond
  292.8 32.0 %copy-start.11 = (bf16[1024,384]{1,0:T(8,128)(2,1)S(1)}, bf16[1024,384]{1,0:T(8,128)(2,1)}, u32[]{:S(2)}) copy-start(bf16[1024,384]{1,0:T(8,128)(2,1)} %copy-done.10) | copy-start | bytes 2359300 | tf_op jit(solution)/shard_map/cond
  317.2 27.2 %all-to-all-start.1 = ((bf16[16,64,384]{2,1,0:T(8,128)(2,1)}), bf16[16,64,384]{2,1,0:T(8,128)(2,1)S(1)}, u32[]{:S(2)}, u32[]{:S(2)}) async-start(bf16[16,64,384]{2,1,0:T(8,128)(2,1)} %bitcast.118), calls=%async_computation.1 | async-start | bytes 1572864 | tf_op jit(solution)/shard_map/cond/branch_1_fun/all_to_all | solution.py:630
  344.5 1.9 collective-permute-start.1
  423.7 37.0 %collective-permute-start.2 = (bf16[16,152,384]{2,1,0:T(8,128)(2,1)S(1)}, bf16[16,152,384]{2,1,0:T(8,128)(2,1)}, u32[]{:S(2)}, u32[]{:S(2)}) collective-permute-start(bf16[16,152,384]{2,1,0:T(8,128)(2,1)S(1)} %all_to_all.55), channel_id=1, source_target_pairs={{0,1},{1,0},{2,3},{3,2},{4,5},{5,4},{6,7},{7,6},{8,9},{9,8},{10,11... | collective-permute-start | bytes 5603336 | tf_op jit(solution)/shard_map/cond/branch_1_fun/ppermute | solution.py:655
  433.4 24.3 %all-to-all-start.4 = ((bf16[16,64,384]{2,1,0:T(8,128)(2,1)}), bf16[16,64,384]{2,1,0:T(8,128)(2,1)}, u32[]{:S(2)}, u32[]{:S(2)}) async-start(bf16[16,64,384]{2,1,0:T(8,128)(2,1)} %bitcast.17), calls=%async_computation.4 | async-start | bytes 1572864 | tf_op jit(solution)/shard_map/cond/branch_1_fun/all_to_all | solution.py:630
  (16 other events, 66.3 us)
Sparse Core Ops, SparseCore 0:
  204.9 169.8 all-reduce.3
